TPU v7x, 32 devices: a whole 2x2x4 slice. The times are simulated.
32 devices in a mesh: row: 4 (over y, core), col: 8 (over z, x).
Axes of the slice: x: 2, y: 2, z: 4, core: 2. Of those that a mesh axis runs over, the one named last changes fastest.
Arguments:
- density: float32 [4, 8, 7, 2, 128, 128], P('row', 'col'), may hold values from -1 to 2, as said below
- hamiltonian: float32 [4, 8, 7, 2, 128, 128], P('row', 'col'), may hold values from -2 to 4, as said below
- offsets: int32 [7, 3], replicated, may hold values from -1 to 1, as said below
- branch: int32 [3], replicated, may hold values from 0 to 1, as said below
Outputs:
- new_density: float32 [4, 8, 7, 2, 128, 128], P('row', 'col')
- grad_density: float32 [4, 8, 7, 2, 128, 128], P('row', 'col')
- totals: float32 [2], replicated
Inputs may be any that keep to these rules, and one draw needn't show every extreme that they name: 7 distinct offsets; (0, 0, 0) is one of them and with each offset its negative (layer step modulo 2) is another; row and column steps lie in -1 to 1, and nonzero row steps and nonzero column steps both occur. `branch`: each entry is 0 or 1, and not all entries are equal. `density`: the matrix is symmetric: entry [p, q, t, s] is the transpose of the entry of the opposite offset at the transposed block position. `hamiltonian`: the matrix is symmetric, in the same sense as the density.
All inputs are finite; a program needn't handle non-finite values.
Results may differ from a plain program's by a relative error of at most 0.0003.
Values sent between devices are 32-bit elements; how exact they have to be, the bound alone decides.
No kernel may reach another device: no remote copies, remote signals or barrier semaphores. Data moves between devices by JAX's collectives and lax.ppermute only.
A program may use at most 128 MiB of HBM per device.

v0:
```python
import types

import jax
import jax.numpy as jnp
from jax import lax
from jax.experimental import pallas as pl
from jax.experimental.pallas import tpu as pltpu
from jax.sharding import PartitionSpec as P

F32 = jnp.float32
BF16 = jnp.bfloat16
EXTRA = 8
SIDES = ("col_far", "col_near", "row_near", "row_far")


def each(count, body, rolled):
    if not rolled:
        for i in range(count):
            body(i)
        return

    def step(i, carry):
        body(i)
        return carry

    lax.fori_loop(0, count, step, 0)


def total_of(count, term, first, rolled):
    if not rolled:
        for i in range(count):
            first = first + term(i)
        return first
    return lax.fori_loop(0, count, lambda i, sum_: sum_ + term(i), first)


def iotas(size):
    shape = (size, size)
    return lax.broadcasted_iota(jnp.int32, shape, 0), lax.broadcasted_iota(jnp.int32, shape, 1)


def store_split(dst, index, value):
    size = value.shape[-1]
    high = value.astype(BF16)
    dst[index + (slice(None), slice(0, size))] = high
    dst[index + (slice(None), slice(size, 2 * size))] = (value - high.astype(F32)).astype(BF16)


def split_all(src, dst, rolled):
    layers = src.shape[1]

    def one(i):
        t, s = i // layers, i % layers
        store_split(dst, (t, s), src[t, s])

    each(src.shape[0] * layers, one, rolled)


def quadrants(q):
    size = q.shape[-1] // 2
    return (q[:size, :size] + q[size:, size:]) + (q[:size, size:] + q[size:, :size])


def edge_product(lefts, rights):
    size = lefts[0].shape[0]
    high = [x[:, :size] for x in lefts]
    low = [x[:, size:] for x in lefts]
    lhs = jnp.concatenate([jnp.concatenate(high, 1), jnp.concatenate(low, 1)], 0)
    rhs = jnp.concatenate(rights, 0)
    return quadrants(jnp.dot(lhs, rhs, preferred_element_type=F32))


def turned(value):
    size = value.shape[0]
    parts = [value[:, :size], value[:, size:]]
    return jnp.concatenate([x.astype(F32).T.astype(BF16) for x in parts], 1)


def symmetric(value):
    return value + value.T


def pack_pair(first, second):
    size = first.shape[-1]
    row, col = iotas(size)
    body = jnp.where(row <= col, first, second)
    diagonal = jnp.sum(jnp.where(row == col, second, 0.0), axis=0, keepdims=True)
    return jnp.concatenate([body, jnp.broadcast_to(diagonal, (EXTRA, size))], axis=0)


def unpack_pair(packed):
    size = packed.shape[-1]
    row, col = iotas(size)
    body = packed[:size]
    other = body.T
    second_diagonal = packed[size : size + 1]
    first = jnp.where(row <= col, body, other)
    second = jnp.where(row > col, body, jnp.where(row == col, second_diagonal, other))
    return first, second


def put_pairs(ref, which, blocks):
    for k in range(len(blocks) // 2):
        ref[which, k] = pack_pair(blocks[2 * k], blocks[2 * k + 1])


def put_row(refs, value):
    size = value.shape[-1]
    for ref in refs:
        ref[0, 0, size + 1 : size + 2, :] = value


def get_row(ref):
    size = ref.shape[-1]
    return ref[0, 0, size + 1 : size + 2, :]


def odd(axis):
    return lax.rem(lax.axis_index(axis), 2)


def wrap(layer, layers):
    return lax.rem(layer + 2 * layers, layers)


def slot_offsets(off, t, layers):
    return off[t, 0], off[t, 1], lax.rem(off[t, 2] + layers, layers)


def zero_slot(off, slots):
    z = jnp.int32(0)
    for t in range(slots):
        hit = (off[t, 0] == 0) & (off[t, 1] == 0) & (off[t, 2] == 0)
        z = jnp.where(hit, jnp.int32(t), z)
    return z


def sign_of(branch, k):
    return (2 * branch[k] - 1).astype(F32)


def closes(off, slots, layers, rows, cols):
    def code(r, c, l):
        return (r + 1) * (3 * layers) + (c + 1) * layers + l

    held = jnp.int32(0)
    places = []
    for t in range(slots):
        r, c, l = slot_offsets(off, t, layers)
        nonzero = (r != 0) | (c != 0) | (l != 0)
        held = held | jnp.where(nonzero, jnp.left_shift(jnp.int32(1), code(r, c, l)), 0)
        places.append((r, c, l, nonzero))
    found = jnp.int32(0)
    for i in range(slots):
        for j in range(i + 1):
            (r, c, l, some), (r2, c2, l2, some2) = places[i], places[j]
            r3 = lax.rem(r + r2 + 1 + rows, rows) - 1
            c3 = lax.rem(c + c2 + 1 + cols, cols) - 1
            l3 = lax.rem(l + l2, layers)
            inside = (r3 <= 1) & (c3 <= 1) & some & some2
            place = jnp.where(inside, code(r3, c3, l3), 0)
            hit = jnp.right_shift(held, place) & 1
            found = found | jnp.where(inside, hit, 0)
    return found


def triangle(off, slots, layers):
    def find(test):
        place = jnp.int32(0)
        for t in range(slots):
            place = jnp.where(test(off[t, 0], off[t, 1]), jnp.int32(t), place)
        return place

    g = types.SimpleNamespace()
    g.a = [find(lambda r, c, d=d: (r == d) & (c == 0)) for d in (-1, 1)]
    g.c = [find(lambda r, c, d=d: (r == d) & (c != 0)) for d in (-1, 1)]
    g.beta = off[g.c[1], 1]
    g.b = [find(lambda r, c, d=d: (r == 0) & (c == d * g.beta)) for d in (-1, 1)]
    g.la, g.lb, g.lc = (lax.rem(off[x[1], 2] + layers, layers) for x in (g.a, g.b, g.c))
    return g


def pick(pair, index):
    return jnp.where(index > 0, pair[1], pair[0])


def vertex_sums(off, left, right, acc, rolled):
    slots, layers = left.shape[0], left.shape[1]
    acc[...] = jnp.zeros_like(acc)

    def add(i):
        t, s = i // layers, i % layers
        r, _, l = slot_offsets(off, t, layers)
        q = lax.dot_general(
            left[t, s], right[t, s], (((0,), (0,)), ((), ())), preferred_element_type=F32
        )
        acc[r + 1, lax.rem(s + l, layers)] += quadrants(q)

    each(slots * layers, add, rolled)


def send_sums(acc, which, near, far, sym):
    layers = acc.shape[1]
    parity = odd("row")
    for r, ref in ((2 - 2 * parity, near), (2 * parity, far)):
        blocks = [acc[r, s] for s in range(layers)]
        put_pairs(ref, which, [symmetric(b) for b in blocks] if sym else blocks)


def add_sums(value, near, far, which):
    out = list(value)
    for k in range(len(out) // 2):
        for message in (near, far):
            first, second = unpack_pair(message[which, k])
            out[2 * k] = out[2 * k] + first
            out[2 * k + 1] = out[2 * k + 1] + second
    return out


def fill_neighbours(dst, own, near, far, parity, blocks):
    for k in range(dst.shape[1] // 2):
        for slot, message in ((2 - 2 * parity, near), (2 * parity, far)):
            first, second = blocks(message, k)
            store_split(dst, (slot, 2 * k), first)
            store_split(dst, (slot, 2 * k + 1), second)
    for s in range(dst.shape[1]):
        store_split(dst, (1, s), own[s])


def diagonal_blocks(k, name, own, rows, cols, which):
    def blocks(message, pair):
        return unpack_pair(message[which, pair])

    side = messages(k, name)
    fill_neighbours(rows, own, side["row_near"], side["row_far"], odd("row"), blocks)
    fill_neighbours(cols, own, side["col_near"], side["col_far"], odd("col"), blocks)


def messages(k, name):
    return {side: getattr(k, name + "_" + side) for side in SIDES}


def closed_send(k, out, f32, left, right, cross, sums_at, edges_at):
    slots, layers = left.shape[0], left.shape[1]
    g = triangle(k.off, slots, layers)
    side = messages(k, out)

    def two(x, y):
        lefts, rights = x(left), y(right)
        if not cross:
            return edge_product([lefts], [rights])
        return edge_product([lefts, x(right)], [rights, y(left)])

    parity = odd("row")
    for index, ref in ((1 - parity, side["row_near"]), (parity, side["row_far"])):
        d = 2 * index - 1
        b, c, other = pick(g.b, index), pick(g.c, index), pick(g.b, 1 - index)

        def row_blocks(s, ref=ref, d=d, b=b, c=c, other=other):
            m = wrap(s - d * g.lc, layers)
            if sums_at is not None:
                ref[sums_at, s] = two(lambda x: turned(x[c, m]), lambda x: x[b, m])
            if edges_at is not None:
                ref[edges_at, s] = f32[other, s]

        each(layers, row_blocks, True)
    parity = odd("col")
    for d, ref in ((1 - 2 * parity, side["col_near"]), (2 * parity - 1, side["col_far"])):
        sigma = d * g.beta
        index = (sigma + 1) // 2
        a, other, c = pick(g.a, index), pick(g.a, 1 - index), pick(g.c, 1 - index)

        def col_blocks(s, ref=ref, sigma=sigma, a=a, other=other, c=c):
            m = wrap(s + sigma * g.lb, layers)
            if sums_at is not None:
                ref[sums_at, s] = two(lambda x: x[other, s], lambda x: turned(x[c, m]))
            if edges_at is not None:
                ref[edges_at, s] = f32[a, s]

        each(layers, col_blocks, True)


def closed_edges(k, name, near_a, near_b, value):
    layers = near_a.shape[1]
    g = triangle(k.off, k.off.shape[0], layers)
    side = messages(k, name)
    parity = odd("row")
    for index, key in ((1 - parity, "row_near"), (parity, "row_far")):
        each(
            layers,
            lambda s, i=index, key=key: store_split(near_b, (i, s), value(side[key], key, s)),
            True,
        )
    parity = odd("col")
    for d, key in ((1 - 2 * parity, "col_near"), (2 * parity - 1, "col_far")):
        index = (1 - d * g.beta) // 2
        each(
            layers,
            lambda s, i=index, key=key: store_split(near_a, (i, s), value(side[key], key, s)),
            True,
        )


def closed_terms(k, name, terms, value, lefts, rights):
    layers = terms.shape[1]
    g = triangle(k.off, k.off.shape[0], layers)
    side = messages(k, name)
    parity = odd("row")
    for index, key in ((1 - parity, "row_near"), (parity, "row_far")):
        for s in range(layers):
            k.came_a[index, s] = value(side[key], key, s)
    parity = odd("col")
    for d, key in ((1 - 2 * parity, "col_near"), (2 * parity - 1, "col_far")):
        index = (1 - d * g.beta) // 2
        for s in range(layers):
            k.came_b[index, s] = value(side[key], key, s)

    def product(x, y):
        return edge_product([x(*left) for left in lefts], [y(*right) for right in rights])

    def corner(i):
        index, s = i // layers, i % layers
        sigma = 2 * index - 1
        a, b, c = pick(g.a, index), pick(g.b, index), pick(g.c, index)
        back, on, up = (wrap(s + m, layers) for m in (-sigma * g.lb, sigma * g.lb, sigma * g.la))
        terms[a, s] = k.came_a[index, s] + product(
            lambda f, ea, eb: turned(f[b, back]), lambda f, ea, eb: f[c, back]
        )
        terms[b, s] = k.came_b[index, s] + product(
            lambda f, ea, eb: f[c, s], lambda f, ea, eb: turned(f[a, on])
        )
        terms[c, s] = product(lambda f, ea, eb: f[b, s], lambda f, ea, eb: f[a, on]) + product(
            lambda f, ea, eb: ea[index, s], lambda f, ea, eb: eb[index, up]
        )

    each(2 * layers, corner, True)


def start_kernel(rows, cols, k):
    slots, layers = k.x.shape[0], k.x.shape[1]
    z = zero_slot(k.off, slots)
    for t in range(slots):
        for j in range(3):
            k.table[t, j] = k.off[t, j]
    k.flag[0] = closes(k.off, slots, layers, rows, cols)
    split_all(k.x, k.xs, False)
    vertex_sums(k.off, k.xs, k.xs, k.acc, False)
    for ref in (k.near, k.far, k.side):
        put_pairs(ref, 0, [k.x[z, s] for s in range(layers)])
        put_pairs(ref, 1, [k.h[z, s] for s in range(layers)])
    send_sums(k.acc, 2, k.near, k.far, False)
    for s in range(layers):
        k.local[s] = k.acc[1, s]


def closed_start_kernel(k):
    split_all(k.x, k.xs, True)
    closed_send(k, "out", k.x, k.xs, k.xs, False, 0, 1)
    closed_send(k, "out", k.h, k.xs, k.xs, False, None, 2)


def square_step(k, step, sums_at, closed):
    slots, layers = k.x.shape[0], k.x.shape[1]
    s_k = sign_of(k.branch, step)
    z = zero_slot(k.off, slots)
    split_all(k.x, k.xs, closed)
    own = [k.x[z, s] for s in range(layers)]
    diagonal_blocks(k, "m", own, k.x_rows, k.x_cols, 0)
    square = add_sums([k.x_local[s] for s in range(layers)], k.m_row_near, k.m_row_far, sums_at)
    for s in range(layers):
        k.new[z, s] = own[s] + s_k * (own[s] - square[s])
    if closed:
        closed_edges(k, "e", k.x_near_a, k.x_near_b, lambda ref, key, s: ref[1, s])
        operand = [(k.xs, k.x_near_a, k.x_near_b)]
        closed_terms(k, "e", k.terms, lambda ref, key, s: ref[0, s], operand, operand)

    def edge(i):
        i, s = i // layers, i % layers
        t = i + (i >= z).astype(jnp.int32)
        r, c, l = slot_offsets(k.off, t, layers)
        e = k.xs[t, s]
        product = edge_product([k.x_cols[1 - c, s], e], [e, k.x_rows[1 + r, lax.rem(s + l, layers)]])
        if closed:
            product = product + k.terms[t, s]
        e32 = k.x[t, s]
        k.new[t, s] = e32 + s_k * (e32 - product)

    each((slots - 1) * layers, edge, closed)
    return z


def square_kernel(step, sums_at, closed, k):
    layers = k.x.shape[1]
    z = square_step(k, step, sums_at, closed)
    for ref in (k.near, k.far, k.side):
        put_pairs(ref, 0, [k.new[z, s] for s in range(layers)])
    split_all(k.new, k.ns, closed)
    vertex_sums(k.off, k.ns, k.ns, k.acc, closed)
    send_sums(k.acc, 1, k.near, k.far, False)
    for s in range(layers):
        k.local[s] = k.acc[1, s]
    if closed:
        closed_send(k, "out", k.new, k.ns, k.ns, False, 0, 1)


def turn_square_kernel(step, sums_at, closed, k):
    square_kernel(step, sums_at, closed, k)
    slots, layers, size = k.x.shape[0], k.x.shape[1], k.x.shape[2]
    z = zero_slot(k.off, slots)
    split_all(k.h, k.hs, closed)
    vertex_sums(k.off, k.hs, k.ns, k.acc_h, closed)
    send_sums(k.acc_h, 2, k.near, k.far, True)
    vertex_sums(k.off, k.ns, k.xs, k.acc_cross, closed)
    send_sums(k.acc_cross, 3, k.near, k.far, True)
    for s in range(layers):
        k.h_local[s] = symmetric(k.acc_h[1, s])
        k.cross_local[s] = symmetric(k.acc_cross[1, s])
    if closed:
        closed_send(k, "out", None, k.hs, k.ns, True, 2, None)
        closed_send(k, "out", None, k.ns, k.xs, True, 3, None)
    s_next = sign_of(k.branch, step + 1)
    row, col = iotas(size)
    squares = total_of(
        slots * layers,
        lambda i: k.new[i // layers, i % layers] * k.new[i // layers, i % layers],
        jnp.zeros((size, size), F32),
        closed,
    )
    trace = jnp.zeros_like(squares)
    for s in range(layers):
        trace = trace + jnp.where(row == col, k.new[z, s], 0.0)
    part = (1.0 + s_next) * trace - s_next * squares
    k.sums[...] = jnp.broadcast_to(jnp.sum(part, keepdims=True), k.sums.shape)
    put_row((k.near, k.far, k.side), k.sums[0:1, :])


def last_square_kernel(step, sums_at, closed, k):
    square_step(k, step, sums_at, closed)
    k.done[...] = jnp.zeros_like(k.done)


def gradient_edges(k, s_k, g, z, closed):
    slots, layers = g.shape[0], g.shape[1]

    def edge(i):
        i, s = i // layers, i % layers
        t = i + (i >= z).astype(jnp.int32)
        r, c, l = slot_offsets(k.off, t, layers)
        e, f = k.gs[t, s], k.xs[t, s]
        b = lax.rem(s + l, layers)
        product = edge_product(
            [k.g_cols[1 - c, s], k.x_cols[1 - c, s], e, f],
            [f, e, k.x_rows[1 + r, b], k.g_rows[1 + r, b]],
        )
        if closed:
            product = product + k.terms[t, s]
        k.new[t, s] = (1.0 + s_k) * g[t, s] - s_k * product

    each((slots - 1) * layers, edge, closed)


def gradient_terms(k, name, value):
    lefts = [(k.gs, k.g_near_a, k.g_near_b), (k.xs, k.x_near_a, k.x_near_b)]
    closed_terms(k, name, k.terms, value, lefts, lefts[::-1])


def gradient_tail(k, z, closed):
    layers = k.x.shape[1]
    for ref in (k.near, k.far, k.side):
        put_pairs(ref, 0, [k.new[z, s] for s in range(layers)])
    split_all(k.new, k.ns, closed)
    split_all(k.before, k.bs, closed)
    vertex_sums(k.off, k.ns, k.bs, k.acc, closed)
    send_sums(k.acc, 1, k.near, k.far, True)
    for s in range(layers):
        k.local[s] = symmetric(k.acc[1, s])
    if closed:
        closed_send(k, "out", k.new, k.ns, k.bs, True, 0, 1)


def first_gradient_kernel(step, four, closed, k):
    layers = k.x.shape[1]
    s_k = sign_of(k.branch, step)
    z = zero_slot(k.off, k.x.shape[0])
    split_all(k.h, k.gs, closed)
    split_all(k.x, k.xs, closed)
    own_h = [k.h[z, s] for s in range(layers)]
    diagonal_blocks(k, "h", own_h, k.g_rows, k.g_cols, 1)
    diagonal_blocks(k, "m", [k.x[z, s] for s in range(layers)], k.x_rows, k.x_cols, 0)
    cross = add_sums([k.h_local[s] for s in range(layers)], k.m_row_near, k.m_row_far, 2)
    for s in range(layers):
        k.new[z, s] = (1.0 + s_k) * own_h[s] - s_k * cross[s]
    if closed:
        closed_edges(k, "he", k.g_near_a, k.g_near_b, lambda ref, key, s: ref[2, s])
        closed_edges(k, "e", k.x_near_a, k.x_near_b, lambda ref, key, s: ref[1, s])
        gradient_terms(k, "e", lambda ref, key, s: ref[2, s])
    gradient_edges(k, s_k, k.h, z, closed)
    gradient_tail(k, z, closed)

    def weigh(i):
        t, s = i // layers, i % layers
        return ((1.0 + s_k) * k.h[t, s] + k.new[t, s]) * k.x[t, s]

    energy = total_of(k.x.shape[0] * layers, weigh, jnp.zeros_like(k.x[0, 0]), closed)
    k.sums[0:1, :] = row_sum(
        four, k.occupied[0:1, :], get_row(k.m_row_near), get_row(k.m_row_far), k.rest[0:1, :]
    )
    k.sums[1:2, :] = jnp.broadcast_to(0.5 * jnp.sum(energy, keepdims=True), (1, k.sums.shape[1]))
    k.sums[2:, :] = jnp.zeros_like(k.sums[2:, :])


def next_gradient_kernel(step, order, closed, k):
    slots, layers, size = k.x.shape[0], k.x.shape[1], k.x.shape[2]
    s_k = sign_of(k.branch, step)
    s_after = sign_of(k.branch, step + 1)
    sums = k.sums[...] + k.done[...]
    k.passed[...] = sums
    excess = sums[0:1, :] * (1.0 / order) - 0.5
    z = zero_slot(k.off, slots)
    row, col = iotas(size)
    eye = jnp.where(row == col, excess * (1.0 + s_after), 0.0)
    scale = excess * (-2.0 * s_after)

    def assemble(i):
        t, s = i // layers, i % layers
        k.g[t, s] = k.gh[t, s] + scale * k.after[t, s]

    each(slots * layers, assemble, closed)
    for s in range(layers):
        k.g[z, s] = k.g[z, s] + eye
    split_all(k.g, k.gs, closed)
    split_all(k.x, k.xs, closed)
    own_g = [k.g[z, s] for s in range(layers)]
    own_x = [k.x[z, s] for s in range(layers)]

    def blocks(message, pair):
        now, then = (unpack_pair(m[0, pair]) for m in message)
        return [a + scale * b + eye for a, b in zip(now, then)]

    gm, am = messages(k, "gm"), messages(k, "am")
    both = {side: (gm[side], am[side]) for side in SIDES}
    fill_neighbours(k.g_rows, own_g, both["row_near"], both["row_far"], odd("row"), blocks)
    fill_neighbours(k.g_cols, own_g, both["col_near"], both["col_far"], odd("col"), blocks)
    diagonal_blocks(k, "m", own_x, k.x_rows, k.x_cols, 0)
    own_sums = add_sums([k.g_local[s] for s in range(layers)], k.gm_row_near, k.gm_row_far, 1)
    cross_sums = add_sums([k.cross_local[s] for s in range(layers)], k.am_row_near, k.am_row_far, 3)
    twice = 2.0 * (1.0 + s_after) * excess
    for s in range(layers):
        cross = own_sums[s] + scale * cross_sums[s] + twice * own_x[s]
        k.new[z, s] = (1.0 + s_k) * own_g[s] - s_k * cross
    if closed:
        ae = messages(k, "ae")
        closed_edges(
            k, "ge", k.g_near_a, k.g_near_b, lambda ref, key, s: ref[1, s] + scale * ae[key][1, s]
        )
        closed_edges(k, "e", k.x_near_a, k.x_near_b, lambda ref, key, s: ref[1, s])
        gradient_terms(k, "ge", lambda ref, key, s: ref[0, s] + scale * ae[key][3, s])
    gradient_edges(k, s_k, k.g, z, closed)
    gradient_tail(k, z, closed)
    k.energy[...] = jnp.broadcast_to(sums[1:2, :], k.energy.shape)
    put_row((k.near, k.far, k.side), sums[1:2, :])


def last_gradient_kernel(step, order, four, closed, k):
    layers = k.x.shape[1]
    s_k = sign_of(k.branch, step)
    z = zero_slot(k.off, k.x.shape[0])
    split_all(k.g, k.gs, closed)
    split_all(k.x, k.xs, closed)
    own_g = [k.g[z, s] for s in range(layers)]
    diagonal_blocks(k, "gm", own_g, k.g_rows, k.g_cols, 0)
    diagonal_blocks(k, "m", [k.x[z, s] for s in range(layers)], k.x_rows, k.x_cols, 0)
    cross = add_sums([k.g_local[s] for s in range(layers)], k.gm_row_near, k.gm_row_far, 1)
    for s in range(layers):
        k.new[z, s] = (1.0 + s_k) * own_g[s] - s_k * cross[s]
    if closed:
        closed_edges(k, "ge", k.g_near_a, k.g_near_b, lambda ref, key, s: ref[1, s])
        closed_edges(k, "e", k.x_near_a, k.x_near_b, lambda ref, key, s: ref[1, s])
        gradient_terms(k, "ge", lambda ref, key, s: ref[0, s])
    gradient_edges(k, s_k, k.g, z, closed)
    energy = row_sum(four, k.energy[...], get_row(k.gm_row_near), get_row(k.gm_row_far), k.rest[...])
    lane = lax.broadcasted_iota(jnp.int32, k.totals.shape, 1)
    k.totals[...] = jnp.where(lane == 0, energy, k.sums[0:1, :]) * (1.0 / order)


def call(kernel, smem, vmem, outs, scratch, smem_outs=()):
    names = [*smem, *vmem, *outs, *dict(smem_outs), *scratch]
    small = dict(smem_outs)

    def body(*refs):
        kernel(types.SimpleNamespace(**dict(zip(names, refs))))

    results = pl.pallas_call(
        body,
        out_shape=[jax.ShapeDtypeStruct(shape, F32) for shape in outs.values()]
        + [jax.ShapeDtypeStruct(shape, jnp.int32) for shape in small.values()],
        in_specs=[pl.BlockSpec(memory_space=pltpu.SMEM)] * len(smem)
        + [pl.BlockSpec(memory_space=pltpu.VMEM)] * len(vmem),
        out_specs=[pl.BlockSpec(memory_space=pltpu.VMEM)] * len(outs)
        + [pl.BlockSpec(memory_space=pltpu.SMEM)] * len(small),
        scratch_shapes=list(scratch.values()),
        compiler_params=pltpu.CompilerParams(vmem_limit_bytes=40 * 1024 * 1024),
    )(*smem.values(), *vmem.values())
    return types.SimpleNamespace(**dict(zip([*outs, *small], results)))


def pairs_of(axis):
    count = lax.axis_size(axis)
    near = [(i, i ^ 1) for i in range(count)]
    far = [(i, (i - 1) % count if i % 2 == 0 else (i + 1) % count) for i in range(count)]
    return near, far


def swap(col_far, col_near, row_near, row_far):
    near_row, far_row = pairs_of("row")
    near_col, far_col = pairs_of("col")
    return dict(
        col_far=lax.ppermute(col_far, "col", far_col),
        col_near=lax.ppermute(col_near, "col", near_col),
        row_near=lax.ppermute(row_near, "row", near_row),
        row_far=lax.ppermute(row_far, "row", far_row),
    )


def exchange(k):
    return swap(k.side, k.side, k.near, k.far)


def exchange_edges(k):
    return swap(k.out_col_far, k.out_col_near, k.out_row_near, k.out_row_far)


def named(name, arrays):
    return {name + "_" + side: arrays[side] for side in SIDES}


def total_over(value, axis):
    count = lax.axis_size(axis)
    if count & (count - 1):
        return lax.psum(value, axis)
    step = 1
    while step < count:
        value = value + lax.ppermute(value, axis, [(i, i ^ step) for i in range(count)])
        step *= 2
    return value


def four_rows():
    return lax.axis_size("row") == 4


def row_remainder(value):
    if four_rows():
        return lax.ppermute(value, "row", [(i, i ^ 2) for i in range(4)])
    return total_over(value, "row")


def row_sum(four, own, near, far, rest):
    return (own + near) + (far + rest) if four else rest


class Shapes:
    def __init__(self, density):
        slots, layers, size = density.shape[2:5]
        self.full = (slots, layers, size, size)
        self.local = (layers, size, size)
        self.tile = (8, size)
        self.order = float(size * layers * lax.axis_size("row") * lax.axis_size("col"))
        self.split = pltpu.VMEM((slots, layers, size, 2 * size), BF16)
        self.three = pltpu.VMEM((3, layers, size, 2 * size), BF16)
        self.two = pltpu.VMEM((2, layers, size, 2 * size), BF16)
        self.two_wide = pltpu.VMEM((2, layers, size, size), F32)
        self.acc = pltpu.VMEM((3, layers, size, size), F32)
        self.wide = pltpu.VMEM(self.full, F32)
        self.pairs = (layers // 2, size + EXTRA, size)

    def messages(self, rows, cols):
        return dict(near=(rows, *self.pairs), far=(rows, *self.pairs), side=(cols, *self.pairs))

    def edges(self, count, closed):
        return {"out_" + side: (count, *self.local) for side in SIDES} if closed else {}

    def near_edges(self, names, closed):
        if not closed:
            return {}
        out = dict(terms=self.wide, came_a=self.two_wide, came_b=self.two_wide)
        for name in names:
            out[name + "_near_a"] = self.two
            out[name + "_near_b"] = self.two
        return out


def steps(closed, density, hamiltonian, table, branch, local0, near0):
    shape = Shapes(density)
    x0 = density.reshape(shape.full)
    h = hamiltonian.reshape(shape.full)
    full, local, tile, order = shape.full, shape.local, shape.tile, shape.order
    split, three, acc = shape.split, shape.three, shape.acc
    smem = dict(off=table, branch=branch)
    four = four_rows()
    square_scratch = dict(xs=split, x_rows=three, x_cols=three, **shape.near_edges(["x"], closed))
    pair_scratch = dict(
        gs=split, xs=split, g_rows=three, g_cols=three, x_rows=three, x_cols=three,
        **shape.near_edges(["g", "x"], closed),
    )
    tail = dict(ns=split, bs=split, acc=acc)

    def edges(**fields):
        out = {}
        for name, arrays in fields.items():
            out.update(named(name, arrays) if closed else {})
        return out

    edge0 = edge1 = edge2 = edge_gh = edge_g1 = None
    if closed:
        k = call(closed_start_kernel, dict(off=table), dict(x=x0, h=h), shape.edges(3, True), dict(xs=split))
        edge0 = exchange_edges(k)
    k = call(
        lambda k: square_kernel(0, 2, closed, k), smem,
        dict(x=x0, x_local=local0, **named("m", near0), **edges(e=edge0)),
        dict(new=full, local=local, **shape.messages(2, 1), **shape.edges(2, closed)),
        dict(ns=split, acc=acc, **square_scratch),
    )
    x1, local1, near1 = k.new, k.local, exchange(k)
    if closed:
        edge1 = exchange_edges(k)
    k = call(
        lambda k: turn_square_kernel(1, 1, closed, k), smem,
        dict(x=x1, x_local=local1, h=h, **named("m", near1), **edges(e=edge1)),
        dict(new=full, local=local, h_local=local, cross_local=local, sums=tile,
             **shape.messages(4, 1), **shape.edges(4, closed)),
        dict(ns=split, hs=split, acc=acc, acc_h=acc, acc_cross=acc, **square_scratch),
    )
    x2, local2, h_local, cross_local, occupied, near2 = (
        k.new, k.local, k.h_local, k.cross_local, k.sums, exchange(k)
    )
    if closed:
        edge2 = exchange_edges(k)
    rest = row_remainder(occupied)
    k = call(
        lambda k: first_gradient_kernel(2, four, closed, k), smem,
        dict(h=h, x=x2, before=x1, h_local=h_local, **named("h", near0), **named("m", near2),
             occupied=occupied, rest=rest, **edges(he=edge0, e=edge2)),
        dict(new=full, local=local, sums=tile, **shape.messages(2, 1), **shape.edges(2, closed)),
        dict(**pair_scratch, **tail),
    )
    gh, gh_local, sums, near_gh = k.new, k.local, k.sums, exchange(k)
    if closed:
        edge_gh = exchange_edges(k)
    sums = total_over(sums, "col")
    k = call(
        lambda k: last_square_kernel(2, 1, closed, k), smem,
        dict(**named("m", near2), x=x2, x_local=local2, **edges(e=edge2)),
        dict(new=full, done=tile), square_scratch,
    )
    x3, done = k.new, k.done
    k = call(
        lambda k: next_gradient_kernel(1, order, closed, k), smem,
        dict(sums=sums, done=done, gh=gh, after=x2, x=x1, before=x0, g_local=gh_local,
             cross_local=cross_local, **named("gm", near_gh), **named("am", near2), **named("m", near1),
             **edges(ge=edge_gh, ae=edge2, e=edge1)),
        dict(new=full, local=local, passed=tile, energy=tile,
             **shape.messages(2, 1), **shape.edges(2, closed)),
        dict(g=shape.wide, **pair_scratch, **tail),
    )
    g1, g1_local, sums, energy, near_g1 = k.new, k.local, k.passed, k.energy, exchange(k)
    if closed:
        edge_g1 = exchange_edges(k)
    rest = row_remainder(energy)
    k = call(
        lambda k: last_gradient_kernel(0, order, four, closed, k), smem,
        dict(sums=sums, energy=energy, rest=rest, g=g1, x=x0, g_local=g1_local,
             **named("gm", near_g1), **named("m", near0), **edges(ge=edge_g1, e=edge0)),
        dict(new=full, totals=tile), pair_scratch,
    )
    return x3.reshape(density.shape), k.new.reshape(density.shape), k.totals[0, :2]


def local(density, hamiltonian, offsets, branch):
    shape = Shapes(density)
    x0 = density.reshape(shape.full)
    h = hamiltonian.reshape(shape.full)
    rows, cols = lax.axis_size("row"), lax.axis_size("col")
    k = call(
        lambda k: start_kernel(rows, cols, k), dict(off=offsets), dict(x=x0, h=h),
        dict(local=shape.local, **shape.messages(3, 2)), dict(xs=shape.split, acc=shape.acc),
        dict(flag=(1,), table=offsets.shape),
    )
    near0 = exchange(k)
    return lax.cond(
        k.flag[0] > 0, lambda *a: steps(True, *a), lambda *a: steps(False, *a),
        density, hamiltonian, k.table, branch, k.local, near0,
    )


def solution(mesh):
    return jax.shard_map(
        local,
        mesh=mesh,
        in_specs=(
            P("row", "col", None, None, None, None),
            P("row", "col", None, None, None, None),
            P(),
            P(),
        ),
        out_specs=(
            P("row", "col", None, None, None, None),
            P("row", "col", None, None, None, None),
            P(),
        ),
        check_vma=False,
    )
```

profile of v0, /device:TPU:0, one launch (start us, length us, event | category | flops | bytes accessed | tf_op | source)
XLA Modules:
  0.0 77.9 jit_solution(9340467169262482827)
XLA Ops:
  0.6 0.8 copy.13.refs_0_
  1.4 3.3 %shard_map.73 = (f32[2,128,128]{2,1,0:T(8,128)S(1)}, f32[3,1,136,128]{3,2,1,0:T(8,128)S(1)}, f32[3,1,136,128]{3,2,1,0:T(8,128)S(1)}, f32[2,1,136,128]{3,2,1,0:T(...) custom-call(s32[7,3]{1,0:T(8,128)S(1)} %copy.13.refs_0_, f32[7,2,128,128]{3,2,1,0:T(8,128)} %bitcast.15, f32[7,2,128,128]{3,2,1,0:T(8,128)} %bitcast.23), custom_call_target="tpu_custom_call" | custom-call | tf_op jit(solution)/shard_map/pallas_call | solution.py:593
  5.3 2.7 %collective-permute-start.65 = (f32[3,1,136,128]{3,2,1,0:T(8,128)S(1)}, f32[3,1,136,128]{3,2,1,0:T(8,128)S(1)}, u32[]{:S(2)}, u32[]{:S(2)}) collective-permute-start(f32[3,1,136,128]{3,2,1,0:T(8,128)S(1)} %get-tuple-element.148), channel_id=1, source_target_pairs={{0,24},{8,16},{16,8},{24,0},{1,25},{9,17},{17,9},{25,1},{2,26},{10... | collective-permute-start | bytes 626696 | tf_op jit(solution)/shard_map/ppermute | solution.py:621
  7.9 1.5 %collective-permute-start.63 = (f32[2,1,136,128]{3,2,1,0:T(8,128)S(1)}, f32[2,1,136,128]{3,2,1,0:T(8,128)S(1)}, u32[]{:S(2)}, u32[]{:S(2)}) collective-permute-start(f32[2,1,136,128]{3,2,1,0:T(8,128)S(1)} %get-tuple-element.146), channel_id=1, source_target_pairs={{0,1},{1,0},{2,3},{3,2},{4,5},{5,4},{6,7},{7,6},{8,9},{9,8},{10,11... | collective-permute-start | bytes 417800 | tf_op jit(solution)/shard_map/ppermute | solution.py:619
  9.4 3.6 %collective-permute-start.62 = (f32[2,1,136,128]{3,2,1,0:T(8,128)S(1)}, f32[2,1,136,128]{3,2,1,0:T(8,128)S(1)}, u32[]{:S(2)}, u32[]{:S(2)}) collective-permute-start(f32[2,1,136,128]{3,2,1,0:T(8,128)S(1)} %get-tuple-element.146), channel_id=1, source_target_pairs={{0,7},{1,2},{2,1},{3,4},{4,3},{5,6},{6,5},{7,0},{8,15},{9,10},{10,... | collective-permute-start | bytes 417800 | tf_op jit(solution)/shard_map/ppermute | solution.py:618
  13.6 1.9 %collective-permute-done.63 = f32[2,1,136,128]{3,2,1,0:T(8,128)S(1)} collective-permute-done((f32[2,1,136,128]{3,2,1,0:T(8,128)S(1)}, f32[2,1,136,128]{3,2,1,0:T(8,128)S(1)}, u32[]{:S(2)}, u32[]{:S(2)}) %collective-permute-start.63) | collective-permute-done | bytes 139296 | tf_op jit(solution)/shard_map/ppermute | solution.py:619
  15.5 1.9 %collective-permute-done.62 = f32[2,1,136,128]{3,2,1,0:T(8,128)S(1)} collective-permute-done((f32[2,1,136,128]{3,2,1,0:T(8,128)S(1)}, f32[2,1,136,128]{3,2,1,0:T(8,128)S(1)}, u32[]{:S(2)}, u32[]{:S(2)}) %collective-permute-start.62) | collective-permute-done | bytes 139296 | tf_op jit(solution)/shard_map/ppermute | solution.py:618
  17.5 0.6 copy-done.2
  18.1 59.7 %conditional.1 = (f32[1,1,7,2,128,128]{5,4,3,2,1,0:T(8,128)}, f32[1,1,7,2,128,128]{5,4,3,2,1,0:T(8,128)}, f32[2]{0:T(128)}) conditional(s32[]{:T(128)} %bitcast.12, (f32[1,1,7,2,128,128]{5,4,3,2,1,0:T(8,128)S(1)}, s32[7,3]{1,0:T(8,128)S(1)}, s32[3]{0:T(128)S(1)}, f32[2,128,128]{2,1,0:T(8,128)S(1)}, f32[2,1,136,128]{3,2,1,0:T(8,128)S(1)}, ...), branch_computations={%region_0.0_spmd, %region_1.0_spmd} | conditional | flops 3072 | bytes 35182224 | solution.py:790
  18.1 2.5 %branch_0_fun.6 = (f32[7,2,128,128]{3,2,1,0:T(8,128)S(1)}, f32[2,128,128]{2,1,0:T(8,128)S(1)}, f32[2,1,136,128]{3,2,1,0:T(8,128)S(1)}, f32[2,1,136,128]{3,2,1,0:T(8,128)S(1)}, f32[1,1,136,128]{3,2,1,0:T(8,128)S(1)}) custom-call(s32[7,3]{1,0:T(8,128)S(1)} %get-tuple-element.36.refs_0_, s32[3]{0:T(128)S(1)} %get-tuple-element.37.refs_1_, ...), custom_call_target="tpu_custom_call" | custom-call | tf_op jit(solution)/shard_map/cond/branch_0_fun/pallas_call | solution.py:593
  20.7 0.6 collective-permute-start.3
  21.9 3.6 %collective-permute-start = (f32[1,1,136,128]{3,2,1,0:T(8,128)S(1)}, f32[1,1,136,128]{3,2,1,0:T(8,128)S(1)}, u32[]{:S(2)}, u32[]{:S(2)}) collective-permute-start(f32[1,1,136,128]{3,2,1,0:T(8,128)S(1)} %get-tuple-element.47), channel_id=1, source_target_pairs={{0,7},{1,2},{2,1},{3,4},{4,3},{5,6},{6,5},{7,0},{8,15},{9,10},{10,... | collective-permute-start | bytes 208904 | tf_op jit(solution)/shard_map/cond/branch_0_fun/ppermute | solution.py:618
  25.6 3.3 %collective-permute-done.refs_5_.refs_18_ = f32[1,1,136,128]{3,2,1,0:T(8,128)S(1)} collective-permute-done((f32[1,1,136,128]{3,2,1,0:T(8,128)S(1)}, f32[1,1,136,128]{3,2,1,0:T(8,128)S(1)}, u32[]{:S(2)}, u32[]{:S(2)}) %collective-permute-start) | collective-permute-done | bytes 69664 | tf_op jit(solution)/shard_map/cond/branch_0_fun/ppermute | solution.py:618
  28.9 3.8 %branch_0_fun.7 = (f32[7,2,128,128]{3,2,1,0:T(8,128)S(1)}, f32[2,128,128]{2,1,0:T(8,128)S(1)}, f32[2,128,128]{2,1,0:T(8,128)S(1)}, f32[2,128,128]{2,1,0:T(8,128)...) custom-call(s32[7,3]{1,0:T(8,128)S(1)} %get-tuple-element.36.refs_0_, ...), custom_call_target="tpu_custom_call" | custom-call | tf_op jit(solution)/shard_map/cond/branch_0_fun/pallas_call | solution.py:593
  32.8 1.6 %collective-permute-start.7 = (f32[4,1,136,128]{3,2,1,0:T(8,128)S(1)}, f32[4,1,136,128]{3,2,1,0:T(8,128)S(1)}, u32[]{:S(2)}, u32[]{:S(2)}) collective-permute-start(f32[4,1,136,128]{3,2,1,0:T(8,128)S(1)} %get-tuple-element.52), channel_id=1, source_target_pairs={{0,24},{8,16},{16,8},{24,0},{1,25},{9,17},{17,9},{25,1},{2,26},{10... | collective-permute-start | bytes 835592 | tf_op jit(solution)/shard_map/cond/branch_0_fun/ppermute | solution.py:621
  34.4 3.6 %collective-permute-start.4 = (f32[1,1,136,128]{3,2,1,0:T(8,128)S(1)}, f32[1,1,136,128]{3,2,1,0:T(8,128)S(1)}, u32[]{:S(2)}, u32[]{:S(2)}) collective-permute-start(f32[1,1,136,128]{3,2,1,0:T(8,128)S(1)} %get-tuple-element.50), channel_id=1, source_target_pairs={{0,7},{1,2},{2,1},{3,4},{4,3},{5,6},{6,5},{7,0},{8,15},{9,10},{10,... | collective-permute-start | bytes 208904 | tf_op jit(solution)/shard_map/cond/branch_0_fun/ppermute | solution.py:618
  38.5 3.4 %collective-permute-done.8.refs_15_ = f32[8,128]{1,0:T(8,128)S(1)} collective-permute-done((f32[8,128]{1,0:T(8,128)S(1)}, f32[8,128]{1,0:T(8,128)S(1)}, u32[]{:S(2)}, u32[]{:S(2)}) %collective-permute-start.8) | collective-permute-done | bytes 4128 | tf_op jit(solution)/shard_map/cond/branch_0_fun/ppermute | solution.py:654
  41.9 3.4 %branch_0_fun.9 = (f32[7,2,128,128]{3,2,1,0:T(8,128)S(1)}, f32[2,128,128]{2,1,0:T(8,128)S(1)}, f32[8,128]{1,0:T(8,128)S(1)}, f32[2,1,136,128]{3,2,1,0:T(8,128)S(...) custom-call(s32[7,3]{1,0:T(8,128)S(1)} %get-tuple-element.36.refs_0_, ...), custom_call_target="tpu_custom_call" | custom-call | tf_op jit(solution)/shard_map/cond/branch_0_fun/pallas_call | solution.py:593
  45.4 1.6 %collective-permute-start.15 = (f32[2,1,136,128]{3,2,1,0:T(8,128)S(1)}, f32[2,1,136,128]{3,2,1,0:T(8,128)S(1)}, u32[]{:S(2)}, u32[]{:S(2)}) collective-permute-start(f32[2,1,136,128]{3,2,1,0:T(8,128)S(1)} %get-tuple-element.65), channel_id=1, source_target_pairs={{0,24},{8,16},{16,8},{24,0},{1,25},{9,17},{17,9},{25,1},{2,26},{10... | collective-permute-start | bytes 417800 | tf_op jit(solution)/shard_map/cond/branch_0_fun/ppermute | solution.py:621
  47.0 3.6 %collective-permute-start.12 = (f32[1,1,136,128]{3,2,1,0:T(8,128)S(1)}, f32[1,1,136,128]{3,2,1,0:T(8,128)S(1)}, u32[]{:S(2)}, u32[]{:S(2)}) collective-permute-start(f32[1,1,136,128]{3,2,1,0:T(8,128)S(1)} %get-tuple-element.63), channel_id=1, source_target_pairs={{0,7},{1,2},{2,1},{3,4},{4,3},{5,6},{6,5},{7,0},{8,15},{9,10},{10,... | collective-permute-start | bytes 208904 | tf_op jit(solution)/shard_map/cond/branch_0_fun/ppermute | solution.py:618
  50.6 3.6 %collective-permute-done.9 = f32[8,128]{1,0:T(8,128)S(1)} collective-permute-done((f32[8,128]{1,0:T(8,128)S(1)}, f32[8,128]{1,0:T(8,128)S(1)}, u32[]{:S(2)}, u32[]{:S(2)}) %collective-permute-start.9) | collective-permute-done | bytes 4128 | tf_op jit(solution)/shard_map/cond/branch_0_fun/ppermute | solution.py:643
  54.2 3.6 %collective-permute-done.10 = f32[8,128]{1,0:T(8,128)S(1)} collective-permute-done((f32[8,128]{1,0:T(8,128)S(1)}, f32[8,128]{1,0:T(8,128)S(1)}, u32[]{:S(2)}, u32[]{:S(2)}) %collective-permute-start.10) | collective-permute-done | bytes 4128 | tf_op jit(solution)/shard_map/cond/branch_0_fun/ppermute | solution.py:643
  58.4 2.6 %branch_0_fun.8 = (f32[7,2,128,128]{3,2,1,0:T(8,128)}, f32[8,128]{1,0:T(8,128)S(1)}) custom-call(s32[7,3]{1,0:T(8,128)S(1)} %get-tuple-element.36.refs_0_, s32[3]{0:T(128)S(1)} %get-tuple-element.37.refs_1_, f32[1,1,136,128]{3,2,1,0:T(8,128)S(1)} %collective-permute-done.4.refs_2_.refs_10_.refs_14_, ...), custom_call_target="tpu_custom_call" | custom-call | tf_op jit(solution)/shard_map/cond/branch_0_fun/pallas_call | solution.py:593
  61.0 1.4 %collective-permute-done.11 = f32[8,128]{1,0:T(8,128)S(1)} collective-permute-done((f32[8,128]{1,0:T(8,128)S(1)}, f32[8,128]{1,0:T(8,128)S(1)}, u32[]{:S(2)}, u32[]{:S(2)}) %collective-permute-start.11) | collective-permute-done | bytes 4128 | tf_op jit(solution)/shard_map/cond/branch_0_fun/ppermute | solution.py:643
  62.4 3.5 %branch_0_fun.10 = (f32[7,2,128,128]{3,2,1,0:T(8,128)S(1)}, f32[2,128,128]{2,1,0:T(8,128)S(1)}, f32[8,128]{1,0:T(8,128)S(1)}, f32[8,128]{1,0:T(8,128)S(1)}, f32[...) custom-call(s32[7,3]{1,0:T(8,128)S(1)} %get-tuple-element.36.refs_0_, ...), custom_call_target="tpu_custom_call" | custom-call | tf_op jit(solution)/shard_map/cond/branch_0_fun/pallas_call | solution.py:593
  66.0 0.6 collective-permute-start.20
  66.6 0.7 collective-permute-start.18
  67.2 1.8 %collective-permute-start.17 = (f32[1,1,136,128]{3,2,1,0:T(8,128)S(1)}, f32[1,1,136,128]{3,2,1,0:T(8,128)S(1)}, u32[]{:S(2)}, u32[]{:S(2)}) collective-permute-start(f32[1,1,136,128]{3,2,1,0:T(8,128)S(1)} %get-tuple-element.70), channel_id=1, source_target_pairs={{0,7},{1,2},{2,1},{3,4},{4,3},{5,6},{6,5},{7,0},{8,15},{9,10},{10,... | collective-permute-start | bytes 208904 | tf_op jit(solution)/shard_map/cond/branch_0_fun/ppermute | solution.py:618
  69.0 1.5 %collective-permute-start.16 = (f32[8,128]{1,0:T(8,128)S(1)}, f32[8,128]{1,0:T(8,128)S(1)}, u32[]{:S(2)}, u32[]{:S(2)}) collective-permute-start(f32[8,128]{1,0:T(8,128)S(1)} %get-tuple-element.67.refs_3_), channel_id=1, source_target_pairs={{0,16},{8,24},{16,0},{24,8},{1,17},{9,25},{17,1},{25,9},{2,18},{10... | collective-permute-start | bytes 12296 | tf_op jit(solution)/shard_map/cond/branch_0_fun/ppermute | solution.py:654
  70.5 2.1 %collective-permute-done.16.refs_4_ = f32[8,128]{1,0:T(8,128)S(1)} collective-permute-done((f32[8,128]{1,0:T(8,128)S(1)}, f32[8,128]{1,0:T(8,128)S(1)}, u32[]{:S(2)}, u32[]{:S(2)}) %collective-permute-start.16) | collective-permute-done | bytes 4128 | tf_op jit(solution)/shard_map/cond/branch_0_fun/ppermute | solution.py:654
  72.6 1.6 %collective-permute-done.17.refs_8_ = f32[1,1,136,128]{3,2,1,0:T(8,128)S(1)} collective-permute-done((f32[1,1,136,128]{3,2,1,0:T(8,128)S(1)}, f32[1,1,136,128]{3,2,1,0:T(8,128)S(1)}, u32[]{:S(2)}, u32[]{:S(2)}) %collective-permute-start.17) | collective-permute-done | bytes 69664 | tf_op jit(solution)/shard_map/cond/branch_0_fun/ppermute | solution.py:618
  74.3 3.1 %branch_0_fun.11 = (f32[7,2,128,128]{3,2,1,0:T(8,128)}, f32[8,128]{1,0:T(8,128)S(1)}) custom-call(s32[7,3]{1,0:T(8,128)S(1)} %get-tuple-element.36.refs_0_, s32[3]{0:T(128)S(1)} %get-tuple-element.37.refs_1_, f32[8,128]{1,0:T(8,128)S(1)} %get-tuple-element.66.refs_2_, f32[8,128]{1,0:T(8,128)S(1)} %get-tuple-element.67.refs_3_, ...), custom_call_target="tpu_custom_call" | custom-call | tf_op jit(solution)/shard_map/cond/branch_0_fun/pallas_call | solution.py:593
  (37 shorter events, 3.2 us)
Async XLA Ops:
  1.4 16.1 %copy-start = (f32[1,1,7,2,128,128]{5,4,3,2,1,0:T(8,128)S(1)}, f32[1,1,7,2,128,128]{5,4,3,2,1,0:T(8,128)}, u32[]{:S(2)}) copy-start(f32[1,1,7,2,128,128]{5,4,3,2,1,0:T(8,128)} %param.6) | copy-start | bytes 2752516
  1.4 16.1 %copy-start.1 = (f32[1,1,7,2,128,128]{5,4,3,2,1,0:T(8,128)S(1)}, f32[1,1,7,2,128,128]{5,4,3,2,1,0:T(8,128)}, u32[]{:S(2)}) copy-start(f32[1,1,7,2,128,128]{5,4,3,2,1,0:T(8,128)} %param.7) | copy-start | bytes 2752516
  4.7 12.7 %collective-permute-start.64 = (f32[3,1,136,128]{3,2,1,0:T(8,128)S(1)}, f32[3,1,136,128]{3,2,1,0:T(8,128)S(1)}, u32[]{:S(2)}, u32[]{:S(2)}) collective-permute-start(f32[3,1,136,128]{3,2,1,0:T(8,128)S(1)} %get-tuple-element.147), channel_id=1, source_target_pairs={{0,8},{8,0},{16,24},{24,16},{1,9},{9,1},{17,25},{25,17},{2,10},{10... | collective-permute-start | bytes 626696 | tf_op jit(solution)/shard_map/ppermute | solution.py:620
  5.3 12.2 %collective-permute-start.65 = (f32[3,1,136,128]{3,2,1,0:T(8,128)S(1)}, f32[3,1,136,128]{3,2,1,0:T(8,128)S(1)}, u32[]{:S(2)}, u32[]{:S(2)}) collective-permute-start(f32[3,1,136,128]{3,2,1,0:T(8,128)S(1)} %get-tuple-element.148), channel_id=1, source_target_pairs={{0,24},{8,16},{16,8},{24,0},{1,25},{9,17},{17,9},{25,1},{2,26},{10... | collective-permute-start | bytes 626696 | tf_op jit(solution)/shard_map/ppermute | solution.py:621
  7.9 7.6 %collective-permute-start.63 = (f32[2,1,136,128]{3,2,1,0:T(8,128)S(1)}, f32[2,1,136,128]{3,2,1,0:T(8,128)S(1)}, u32[]{:S(2)}, u32[]{:S(2)}) collective-permute-start(f32[2,1,136,128]{3,2,1,0:T(8,128)S(1)} %get-tuple-element.146), channel_id=1, source_target_pairs={{0,1},{1,0},{2,3},{3,2},{4,5},{5,4},{6,7},{7,6},{8,9},{9,8},{10,11... | collective-permute-start | bytes 417800 | tf_op jit(solution)/shard_map/ppermute | solution.py:619
  9.4 8.1 %collective-permute-start.62 = (f32[2,1,136,128]{3,2,1,0:T(8,128)S(1)}, f32[2,1,136,128]{3,2,1,0:T(8,128)S(1)}, u32[]{:S(2)}, u32[]{:S(2)}) collective-permute-start(f32[2,1,136,128]{3,2,1,0:T(8,128)S(1)} %get-tuple-element.146), channel_id=1, source_target_pairs={{0,7},{1,2},{2,1},{3,4},{4,3},{5,6},{6,5},{7,0},{8,15},{9,10},{10,... | collective-permute-start | bytes 417800 | tf_op jit(solution)/shard_map/ppermute | solution.py:618
  17.5 0.7 copy-start.2
  20.6 8.3 %collective-permute-start.2 = (f32[2,1,136,128]{3,2,1,0:T(8,128)S(1)}, f32[2,1,136,128]{3,2,1,0:T(8,128)S(1)}, u32[]{:S(2)}, u32[]{:S(2)}) collective-permute-start(f32[2,1,136,128]{3,2,1,0:T(8,128)S(1)} %get-tuple-element.48), channel_id=1, source_target_pairs={{0,8},{8,0},{16,24},{24,16},{1,9},{9,1},{17,25},{25,17},{2,10},{10... | collective-permute-start | bytes 417800 | tf_op jit(solution)/shard_map/cond/branch_0_fun/ppermute | solution.py:620
  20.7 8.2 %collective-permute-start.3 = (f32[2,1,136,128]{3,2,1,0:T(8,128)S(1)}, f32[2,1,136,128]{3,2,1,0:T(8,128)S(1)}, u32[]{:S(2)}, u32[]{:S(2)}) collective-permute-start(f32[2,1,136,128]{3,2,1,0:T(8,128)S(1)} %get-tuple-element.49), channel_id=1, source_target_pairs={{0,24},{8,16},{16,8},{24,0},{1,25},{9,17},{17,9},{25,1},{2,26},{10... | collective-permute-start | bytes 417800 | tf_op jit(solution)/shard_map/cond/branch_0_fun/ppermute | solution.py:621
  21.3 4.3 %collective-permute-start.1 = (f32[1,1,136,128]{3,2,1,0:T(8,128)S(1)}, f32[1,1,136,128]{3,2,1,0:T(8,128)S(1)}, u32[]{:S(2)}, u32[]{:S(2)}) collective-permute-start(f32[1,1,136,128]{3,2,1,0:T(8,128)S(1)} %get-tuple-element.47), channel_id=1, source_target_pairs={{0,1},{1,0},{2,3},{3,2},{4,5},{5,4},{6,7},{7,6},{8,9},{9,8},{10,11... | collective-permute-start | bytes 208904 | tf_op jit(solution)/shard_map/cond/branch_0_fun/ppermute | solution.py:619
  21.9 7.0 %collective-permute-start = (f32[1,1,136,128]{3,2,1,0:T(8,128)S(1)}, f32[1,1,136,128]{3,2,1,0:T(8,128)S(1)}, u32[]{:S(2)}, u32[]{:S(2)}) collective-permute-start(f32[1,1,136,128]{3,2,1,0:T(8,128)S(1)} %get-tuple-element.47), channel_id=1, source_target_pairs={{0,7},{1,2},{2,1},{3,4},{4,3},{5,6},{6,5},{7,0},{8,15},{9,10},{10,... | collective-permute-start | bytes 208904 | tf_op jit(solution)/shard_map/cond/branch_0_fun/ppermute | solution.py:618
  32.7 9.2 %collective-permute-start.6 = (f32[4,1,136,128]{3,2,1,0:T(8,128)S(1)}, f32[4,1,136,128]{3,2,1,0:T(8,128)S(1)}, u32[]{:S(2)}, u32[]{:S(2)}) collective-permute-start(f32[4,1,136,128]{3,2,1,0:T(8,128)S(1)} %get-tuple-element.51), channel_id=1, source_target_pairs={{0,8},{8,0},{16,24},{24,16},{1,9},{9,1},{17,25},{25,17},{2,10},{10... | collective-permute-start | bytes 835592 | tf_op jit(solution)/shard_map/cond/branch_0_fun/ppermute | solution.py:620
  32.8 9.1 %collective-permute-start.7 = (f32[4,1,136,128]{3,2,1,0:T(8,128)S(1)}, f32[4,1,136,128]{3,2,1,0:T(8,128)S(1)}, u32[]{:S(2)}, u32[]{:S(2)}) collective-permute-start(f32[4,1,136,128]{3,2,1,0:T(8,128)S(1)} %get-tuple-element.52), channel_id=1, source_target_pairs={{0,24},{8,16},{16,8},{24,0},{1,25},{9,17},{17,9},{25,1},{2,26},{10... | collective-permute-start | bytes 835592 | tf_op jit(solution)/shard_map/cond/branch_0_fun/ppermute | solution.py:621
  34.4 7.5 %collective-permute-start.5 = (f32[1,1,136,128]{3,2,1,0:T(8,128)S(1)}, f32[1,1,136,128]{3,2,1,0:T(8,128)S(1)}, u32[]{:S(2)}, u32[]{:S(2)}) collective-permute-start(f32[1,1,136,128]{3,2,1,0:T(8,128)S(1)} %get-tuple-element.50), channel_id=1, source_target_pairs={{0,1},{1,0},{2,3},{3,2},{4,5},{5,4},{6,7},{7,6},{8,9},{9,8},{10,11... | collective-permute-start | bytes 208904 | tf_op jit(solution)/shard_map/cond/branch_0_fun/ppermute | solution.py:619
  34.4 7.5 %collective-permute-start.4 = (f32[1,1,136,128]{3,2,1,0:T(8,128)S(1)}, f32[1,1,136,128]{3,2,1,0:T(8,128)S(1)}, u32[]{:S(2)}, u32[]{:S(2)}) collective-permute-start(f32[1,1,136,128]{3,2,1,0:T(8,128)S(1)} %get-tuple-element.50), channel_id=1, source_target_pairs={{0,7},{1,2},{2,1},{3,4},{4,3},{5,6},{6,5},{7,0},{8,15},{9,10},{10,... | collective-permute-start | bytes 208904 | tf_op jit(solution)/shard_map/cond/branch_0_fun/ppermute | solution.py:618
  38.0 3.9 %collective-permute-start.8 = (f32[8,128]{1,0:T(8,128)S(1)}, f32[8,128]{1,0:T(8,128)S(1)}, u32[]{:S(2)}, u32[]{:S(2)}) collective-permute-start(f32[8,128]{1,0:T(8,128)S(1)} %get-tuple-element.57.refs_14_), channel_id=1, source_target_pairs={{0,16},{8,24},{16,0},{24,8},{1,17},{9,25},{17,1},{25,9},{2,18},{10... | collective-permute-start | bytes 12296 | tf_op jit(solution)/shard_map/cond/branch_0_fun/ppermute | solution.py:654
  45.3 17.0 %collective-permute-start.14 = (f32[2,1,136,128]{3,2,1,0:T(8,128)S(1)}, f32[2,1,136,128]{3,2,1,0:T(8,128)S(1)}, u32[]{:S(2)}, u32[]{:S(2)}) collective-permute-start(f32[2,1,136,128]{3,2,1,0:T(8,128)S(1)} %get-tuple-element.64), channel_id=1, source_target_pairs={{0,8},{8,0},{16,24},{24,16},{1,9},{9,1},{17,25},{25,17},{2,10},{10... | collective-permute-start | bytes 417800 | tf_op jit(solution)/shard_map/cond/branch_0_fun/ppermute | solution.py:620
  45.4 17.0 %collective-permute-start.15 = (f32[2,1,136,128]{3,2,1,0:T(8,128)S(1)}, f32[2,1,136,128]{3,2,1,0:T(8,128)S(1)}, u32[]{:S(2)}, u32[]{:S(2)}) collective-permute-start(f32[2,1,136,128]{3,2,1,0:T(8,128)S(1)} %get-tuple-element.65), channel_id=1, source_target_pairs={{0,24},{8,16},{16,8},{24,0},{1,25},{9,17},{17,9},{25,1},{2,26},{10... | collective-permute-start | bytes 417800 | tf_op jit(solution)/shard_map/cond/branch_0_fun/ppermute | solution.py:621
  47.0 15.3 %collective-permute-start.13 = (f32[1,1,136,128]{3,2,1,0:T(8,128)S(1)}, f32[1,1,136,128]{3,2,1,0:T(8,128)S(1)}, u32[]{:S(2)}, u32[]{:S(2)}) collective-permute-start(f32[1,1,136,128]{3,2,1,0:T(8,128)S(1)} %get-tuple-element.63), channel_id=1, source_target_pairs={{0,1},{1,0},{2,3},{3,2},{4,5},{5,4},{6,7},{7,6},{8,9},{9,8},{10,11... | collective-permute-start | bytes 208904 | tf_op jit(solution)/shard_map/cond/branch_0_fun/ppermute | solution.py:619
  47.0 15.3 %collective-permute-start.12 = (f32[1,1,136,128]{3,2,1,0:T(8,128)S(1)}, f32[1,1,136,128]{3,2,1,0:T(8,128)S(1)}, u32[]{:S(2)}, u32[]{:S(2)}) collective-permute-start(f32[1,1,136,128]{3,2,1,0:T(8,128)S(1)} %get-tuple-element.63), channel_id=1, source_target_pairs={{0,7},{1,2},{2,1},{3,4},{4,3},{5,6},{6,5},{7,0},{8,15},{9,10},{10,... | collective-permute-start | bytes 208904 | tf_op jit(solution)/shard_map/cond/branch_0_fun/ppermute | solution.py:618
  50.6 3.6 %collective-permute-start.9 = (f32[8,128]{1,0:T(8,128)S(1)}, f32[8,128]{1,0:T(8,128)S(1)}, u32[]{:S(2)}, u32[]{:S(2)}) collective-permute-start(f32[8,128]{1,0:T(8,128)S(1)} %get-tuple-element.58), channel_id=1, source_target_pairs={{0,1},{1,0},{2,3},{3,2},{4,5},{5,4},{6,7},{7,6},{8,9},{9,8},{10,11... | collective-permute-start | bytes 12296 | tf_op jit(solution)/shard_map/cond/branch_0_fun/ppermute | solution.py:643
  54.2 3.6 %collective-permute-start.10 = (f32[8,128]{1,0:T(8,128)S(1)}, f32[8,128]{1,0:T(8,128)S(1)}, u32[]{:S(2)}, u32[]{:S(2)}) collective-permute-start(f32[8,128]{1,0:T(8,128)S(1)} %add.12), channel_id=1, source_target_pairs={{0,2},{1,3},{2,0},{3,1},{4,6},{5,7},{6,4},{7,5},{8,10},{9,11},{10,... | collective-permute-start | bytes 12296 | tf_op jit(solution)/shard_map/cond/branch_0_fun/ppermute | solution.py:643
  57.8 4.5 %collective-permute-start.11 = (f32[8,128]{1,0:T(8,128)S(1)}, f32[8,128]{1,0:T(8,128)S(1)}, u32[]{:S(2)}, u32[]{:S(2)}) collective-permute-start(f32[8,128]{1,0:T(8,128)S(1)} %add.13), channel_id=1, source_target_pairs={{0,4},{1,5},{2,6},{3,7},{4,0},{5,1},{6,2},{7,3},{8,12},{9,13},{10,... | collective-permute-start | bytes 12296 | tf_op jit(solution)/shard_map/cond/branch_0_fun/ppermute | solution.py:643
  65.9 8.4 %collective-permute-start.19 = (f32[2,1,136,128]{3,2,1,0:T(8,128)S(1)}, f32[2,1,136,128]{3,2,1,0:T(8,128)S(1)}, u32[]{:S(2)}, u32[]{:S(2)}) collective-permute-start(f32[2,1,136,128]{3,2,1,0:T(8,128)S(1)} %get-tuple-element.71), channel_id=1, source_target_pairs={{0,8},{8,0},{16,24},{24,16},{1,9},{9,1},{17,25},{25,17},{2,10},{10... | collective-permute-start | bytes 417800 | tf_op jit(solution)/shard_map/cond/branch_0_fun/ppermute | solution.py:620
  66.0 8.3 %collective-permute-start.20 = (f32[2,1,136,128]{3,2,1,0:T(8,128)S(1)}, f32[2,1,136,128]{3,2,1,0:T(8,128)S(1)}, u32[]{:S(2)}, u32[]{:S(2)}) collective-permute-start(f32[2,1,136,128]{3,2,1,0:T(8,128)S(1)} %get-tuple-element.72), channel_id=1, source_target_pairs={{0,24},{8,16},{16,8},{24,0},{1,25},{9,17},{17,9},{25,1},{2,26},{10... | collective-permute-start | bytes 417800 | tf_op jit(solution)/shard_map/cond/branch_0_fun/ppermute | solution.py:621
  66.6 6.0 %collective-permute-start.18 = (f32[1,1,136,128]{3,2,1,0:T(8,128)S(1)}, f32[1,1,136,128]{3,2,1,0:T(8,128)S(1)}, u32[]{:S(2)}, u32[]{:S(2)}) collective-permute-start(f32[1,1,136,128]{3,2,1,0:T(8,128)S(1)} %get-tuple-element.70), channel_id=1, source_target_pairs={{0,1},{1,0},{2,3},{3,2},{4,5},{5,4},{6,7},{7,6},{8,9},{9,8},{10,11... | collective-permute-start | bytes 208904 | tf_op jit(solution)/shard_map/cond/branch_0_fun/ppermute | solution.py:619
  67.2 7.0 %collective-permute-start.17 = (f32[1,1,136,128]{3,2,1,0:T(8,128)S(1)}, f32[1,1,136,128]{3,2,1,0:T(8,128)S(1)}, u32[]{:S(2)}, u32[]{:S(2)}) collective-permute-start(f32[1,1,136,128]{3,2,1,0:T(8,128)S(1)} %get-tuple-element.70), channel_id=1, source_target_pairs={{0,7},{1,2},{2,1},{3,4},{4,3},{5,6},{6,5},{7,0},{8,15},{9,10},{10,... | collective-permute-start | bytes 208904 | tf_op jit(solution)/shard_map/cond/branch_0_fun/ppermute | solution.py:618
  69.0 3.6 %collective-permute-start.16 = (f32[8,128]{1,0:T(8,128)S(1)}, f32[8,128]{1,0:T(8,128)S(1)}, u32[]{:S(2)}, u32[]{:S(2)}) collective-permute-start(f32[8,128]{1,0:T(8,128)S(1)} %get-tuple-element.67.refs_3_), channel_id=1, source_target_pairs={{0,16},{8,24},{16,0},{24,8},{1,17},{9,25},{17,1},{25,9},{2,18},{10... | collective-permute-start | bytes 12296 | tf_op jit(solution)/shard_map/cond/branch_0_fun/ppermute | solution.py:654
where the time goes:
time: 78.1 us; the launch traced here: 77.9 us
  starting transfers between devices  29.3 us (38%)
  waiting for transfers between devices  23 us (29%)
  Pallas kernels  22.2 us (28%)
  local copies, waits for them, and re-layouts  1.92 us (2%)
  between operations  1.32 us (2%)
    pallas_call x7, Pallas kernels, call(): pl.pallas_call(body, out_shape=[jax.ShapeDtypeStruct(shape, F32) for shap...  22.2 us
    ppermute x5, starting transfers between devices, swap(): lax.ppermute(col_far, 'col', far_col)  16.1 us
    ppermute x3, waiting for transfers between devices, total_over(): lax.ppermute(value, axis, [(i, i ^ step) for i in range(count)])  8.58 us
    ppermute x5, starting transfers between devices, swap(): lax.ppermute(row_far, 'row', far_row)  7.14 us
    ppermute x5, waiting for transfers between devices, swap(): lax.ppermute(col_far, 'col', far_col)  6.82 us
    ppermute x2, waiting for transfers between devices, row_remainder(): return lax.ppermute(value, 'row', [(i, i ^ 2) for i in range(4)])  5.48 us
    ppermute x5, starting transfers between devices, swap(): lax.ppermute(col_near, 'col', near_col)  2.73 us
    ppermute x5, waiting for transfers between devices, swap(): lax.ppermute(col_near, 'col', near_col)  2.08 us
  transfers between devices with their start and end apart: 25, of which 10 were waited for; matrix products, arithmetic and copies ran while one was open for 0% of the time, Pallas kernels for 3%

commit v1 on v0

--- a/solution.py
+++ b/solution.py
@@ -478,7 +478,7 @@
         closed_send(k, "out", k.new, k.ns, k.bs, True, 0, 1)
 
 
-def first_gradient_kernel(step, four, closed, k):
+def first_gradient_kernel(step, closed, k):
     layers = k.x.shape[1]
     s_k = sign_of(k.branch, step)
     z = zero_slot(k.off, k.x.shape[0])
@@ -502,11 +502,7 @@
         return ((1.0 + s_k) * k.h[t, s] + k.new[t, s]) * k.x[t, s]
 
     energy = total_of(k.x.shape[0] * layers, weigh, jnp.zeros_like(k.x[0, 0]), closed)
-    k.sums[0:1, :] = row_sum(
-        four, k.occupied[0:1, :], get_row(k.m_row_near), get_row(k.m_row_far), k.rest[0:1, :]
-    )
-    k.sums[1:2, :] = jnp.broadcast_to(0.5 * jnp.sum(energy, keepdims=True), (1, k.sums.shape[1]))
-    k.sums[2:, :] = jnp.zeros_like(k.sums[2:, :])
+    k.energy[...] = jnp.broadcast_to(0.5 * jnp.sum(energy, keepdims=True), k.energy.shape)
 
 
 def next_gradient_kernel(step, order, closed, k):
@@ -514,7 +510,6 @@
     s_k = sign_of(k.branch, step)
     s_after = sign_of(k.branch, step + 1)
     sums = k.sums[...] + k.done[...]
-    k.passed[...] = sums
     excess = sums[0:1, :] * (1.0 / order) - 0.5
     z = zero_slot(k.off, slots)
     row, col = iotas(size)
@@ -561,7 +556,7 @@
     put_row((k.near, k.far, k.side), sums[1:2, :])
 
 
-def last_gradient_kernel(step, order, four, closed, k):
+def last_gradient_kernel(step, closed, k):
     layers = k.x.shape[1]
     s_k = sign_of(k.branch, step)
     z = zero_slot(k.off, k.x.shape[0])
@@ -578,9 +573,6 @@
         closed_edges(k, "e", k.x_near_a, k.x_near_b, lambda ref, key, s: ref[1, s])
         gradient_terms(k, "ge", lambda ref, key, s: ref[0, s])
     gradient_edges(k, s_k, k.g, z, closed)
-    energy = row_sum(four, k.energy[...], get_row(k.gm_row_near), get_row(k.gm_row_far), k.rest[...])
-    lane = lax.broadcasted_iota(jnp.int32, k.totals.shape, 1)
-    k.totals[...] = jnp.where(lane == 0, energy, k.sums[0:1, :]) * (1.0 / order)
 
 
 def call(kernel, smem, vmem, outs, scratch, smem_outs=()):
@@ -600,6 +592,7 @@
         + [pl.BlockSpec(memory_space=pltpu.SMEM)] * len(small),
         scratch_shapes=list(scratch.values()),
         compiler_params=pltpu.CompilerParams(vmem_limit_bytes=40 * 1024 * 1024),
+        cost_estimate=pl.CostEstimate(flops=2_000_000_000, bytes_accessed=6_000_000, transcendentals=0),
     )(*smem.values(), *vmem.values())
     return types.SimpleNamespace(**dict(zip([*outs, *small], results)))
 
@@ -623,7 +616,9 @@
 
 
 def exchange(k):
-    return swap(k.side, k.side, k.near, k.far)
+    out = swap(k.side, k.side, k.near, k.far)
+    out["first"] = out["row_far"][0, 0, -EXTRA:, :] + out["col_far"][0, 0, -EXTRA:, :]
+    return out
 
 
 def exchange_edges(k):
@@ -634,29 +629,35 @@
     return {name + "_" + side: arrays[side] for side in SIDES}
 
 
-def total_over(value, axis):
+def doubling(value, axis, steps):
+    for step in steps:
+        count = lax.axis_size(axis)
+        value = value + lax.ppermute(value, axis, [(i, i ^ step) for i in range(count)])
+    return value
+
+
+def powers(axis):
     count = lax.axis_size(axis)
-    if count & (count - 1):
-        return lax.psum(value, axis)
-    step = 1
-    while step < count:
-        value = value + lax.ppermute(value, axis, [(i, i ^ step) for i in range(count)])
-        step *= 2
-    return value
-
-
-def four_rows():
-    return lax.axis_size("row") == 4
-
-
-def row_remainder(value):
-    if four_rows():
-        return lax.ppermute(value, "row", [(i, i ^ 2) for i in range(4)])
-    return total_over(value, "row")
-
-
-def row_sum(four, own, near, far, rest):
-    return (own + near) + (far + rest) if four else rest
+    return [] if count & (count - 1) else [1 << i for i in range(count.bit_length() - 1)]
+
+
+def col_first(value):
+    steps = powers("col")
+    return doubling(value, "col", steps[:1]) if steps else lax.psum(value, "col")
+
+
+def col_rest(value):
+    return doubling(value, "col", powers("col")[1:])
+
+
+def row_total(value, came):
+    if lax.axis_size("row") == 4:
+        rest = lax.ppermute(value, "row", [(i, i ^ 2) for i in range(4)])
+        row = value.shape[-1] + 1
+        near, far = (came[side][0, 0, row : row + 1] for side in ("row_near", "row_far"))
+        return (value + near) + (far + rest)
+    steps = powers("row")
+    return doubling(value, "row", steps) if steps else lax.psum(value, "row")
 
 
 class Shapes:
@@ -697,7 +698,6 @@
     full, local, tile, order = shape.full, shape.local, shape.tile, shape.order
     split, three, acc = shape.split, shape.three, shape.acc
     smem = dict(off=table, branch=branch)
-    four = four_rows()
     square_scratch = dict(xs=split, x_rows=three, x_cols=three, **shape.near_edges(["x"], closed))
     pair_scratch = dict(
         gs=split, xs=split, g_rows=three, g_cols=three, x_rows=three, x_cols=three,
@@ -717,7 +717,7 @@
         edge0 = exchange_edges(k)
     k = call(
         lambda k: square_kernel(0, 2, closed, k), smem,
-        dict(x=x0, x_local=local0, **named("m", near0), **edges(e=edge0)),
+        dict(x=x0, x_local=local0, first=near0["first"], **named("m", near0), **edges(e=edge0)),
         dict(new=full, local=local, **shape.messages(2, 1), **shape.edges(2, closed)),
         dict(ns=split, acc=acc, **square_scratch),
     )
@@ -726,7 +726,7 @@
         edge1 = exchange_edges(k)
     k = call(
         lambda k: turn_square_kernel(1, 1, closed, k), smem,
-        dict(x=x1, x_local=local1, h=h, **named("m", near1), **edges(e=edge1)),
+        dict(x=x1, x_local=local1, h=h, first=near1["first"], **named("m", near1), **edges(e=edge1)),
         dict(new=full, local=local, h_local=local, cross_local=local, sums=tile,
              **shape.messages(4, 1), **shape.edges(4, closed)),
         dict(ns=split, hs=split, acc=acc, acc_h=acc, acc_cross=acc, **square_scratch),
@@ -736,18 +736,19 @@
     )
     if closed:
         edge2 = exchange_edges(k)
-    rest = row_remainder(occupied)
+    occupied = col_first(row_total(occupied, near2))
     k = call(
-        lambda k: first_gradient_kernel(2, four, closed, k), smem,
-        dict(h=h, x=x2, before=x1, h_local=h_local, **named("h", near0), **named("m", near2),
-             occupied=occupied, rest=rest, **edges(he=edge0, e=edge2)),
-        dict(new=full, local=local, sums=tile, **shape.messages(2, 1), **shape.edges(2, closed)),
+        lambda k: first_gradient_kernel(2, closed, k), smem,
+        dict(h=h, x=x2, before=x1, h_local=h_local, first=near2["first"], **named("h", near0), **named("m", near2),
+             **edges(he=edge0, e=edge2)),
+        dict(new=full, local=local, energy=tile, **shape.messages(2, 1), **shape.edges(2, closed)),
         dict(**pair_scratch, **tail),
     )
-    gh, gh_local, sums, near_gh = k.new, k.local, k.sums, exchange(k)
+    gh, gh_local, energy, near_gh = k.new, k.local, k.energy, exchange(k)
     if closed:
         edge_gh = exchange_edges(k)
-    sums = total_over(sums, "col")
+    row = lax.broadcasted_iota(jnp.int32, tile, 0)
+    sums = col_rest(jnp.where(row == 0, occupied, energy))
     k = call(
         lambda k: last_square_kernel(2, 1, closed, k), smem,
         dict(**named("m", near2), x=x2, x_local=local2, **edges(e=edge2)),
@@ -756,24 +757,26 @@
     x3, done = k.new, k.done
     k = call(
         lambda k: next_gradient_kernel(1, order, closed, k), smem,
-        dict(sums=sums, done=done, gh=gh, after=x2, x=x1, before=x0, g_local=gh_local,
+        dict(sums=sums, done=done, first=near_gh["first"], gh=gh, after=x2, x=x1, before=x0, g_local=gh_local,
              cross_local=cross_local, **named("gm", near_gh), **named("am", near2), **named("m", near1),
              **edges(ge=edge_gh, ae=edge2, e=edge1)),
-        dict(new=full, local=local, passed=tile, energy=tile,
+        dict(new=full, local=local, energy=tile,
              **shape.messages(2, 1), **shape.edges(2, closed)),
         dict(g=shape.wide, **pair_scratch, **tail),
     )
-    g1, g1_local, sums, energy, near_g1 = k.new, k.local, k.passed, k.energy, exchange(k)
+    g1, g1_local, energy, near_g1 = k.new, k.local, k.energy, exchange(k)
     if closed:
         edge_g1 = exchange_edges(k)
-    rest = row_remainder(energy)
+    energy = col_first(row_total(energy, near_g1))
     k = call(
-        lambda k: last_gradient_kernel(0, order, four, closed, k), smem,
-        dict(sums=sums, energy=energy, rest=rest, g=g1, x=x0, g_local=g1_local,
-             **named("gm", near_g1), **named("m", near0), **edges(ge=edge_g1, e=edge0)),
-        dict(new=full, totals=tile), pair_scratch,
-    )
-    return x3.reshape(density.shape), k.new.reshape(density.shape), k.totals[0, :2]
+        lambda k: last_gradient_kernel(0, closed, k), smem,
+        dict(g=g1, x=x0, g_local=g1_local, first=near_g1["first"], **named("gm", near_g1), **named("m", near0),
+             **edges(ge=edge_g1, e=edge0)),
+        dict(new=full), pair_scratch,
+    )
+    lane = lax.broadcasted_iota(jnp.int32, (2,), 0)
+    totals = jnp.where(lane == 0, energy[0, :2], sums[0, :2]) / order
+    return x3.reshape(density.shape), k.new.reshape(density.shape), totals
 
 
 def local(density, hamiltonian, offsets, branch):

time: 78.1 us -> 73 us (0.935)
  starting transfers between devices: 29.3 us -> 26.4 us
  waiting for transfers between devices: 23 us -> 20.7 us
    ppermute x5 -> x6, waiting for transfers between devices: 14.1 us -> 3.52 us  [the longest x4 2.1 us: doubling(): lax.ppermute(value, axis, [(i, i ^ step) for i in range(count)])]
    ppermute x5, waiting for transfers between devices: 0.01 us -> 4.23 us  [swap(): lax.ppermute(row_far, 'row', far_row)]
    ppermute x5, waiting for transfers between devices: 6.82 us -> 9.46 us  [swap(): lax.ppermute(col_far, 'col', far_col)]
    ppermute x5, starting transfers between devices: 7.14 us -> 4.52 us  [swap(): lax.ppermute(row_far, 'row', far_row)]
    ppermute x5, starting transfers between devices: 0.79 us -> 2.23 us  [swap(): lax.ppermute(row_near, 'row', near_row)]
    ppermute x5, starting transfers between devices: 16.1 us -> 15.1 us  [swap(): lax.ppermute(col_far, 'col', far_col)]
    ppermute x5, waiting for transfers between devices: 2.08 us -> 3.02 us  [swap(): lax.ppermute(col_near, 'col', near_col)]
    ppermute x5 -> x6, starting transfers between devices: 2.59 us -> 2.5 us  [the longest x2 1.99 us: row_total(): rest = lax.ppermute(value, 'row', [(i, i ^ 2) for i in range(4)])]
  transfers between devices with their start and end apart: 25 -> 26, of which waited for: 10 -> 12; matrix products, arithmetic and copies ran while one was open for 0% -> 0% of each run, Pallas kernels for 3% -> 12%
where the time goes in v1:
time: 73 us; the launch traced here: 72.8 us
  starting transfers between devices  26.4 us (36%)
  Pallas kernels  22.2 us (30%)
  waiting for transfers between devices  20.7 us (28%)
  between operations  1.44 us (2%)
  local copies, waits for them, and re-layouts  1.43 us (2%)
    pallas_call x7, Pallas kernels, call(): pl.pallas_call(body, out_shape=[jax.ShapeDtypeStruct(shape, F32) for shap...  22.2 us
    ppermute x5, starting transfers between devices, swap(): lax.ppermute(col_far, 'col', far_col)  15.1 us
    ppermute x5, waiting for transfers between devices, swap(): lax.ppermute(col_far, 'col', far_col)  9.46 us
    ppermute x5, starting transfers between devices, swap(): lax.ppermute(row_far, 'row', far_row)  4.52 us
    ppermute x5, waiting for transfers between devices, swap(): lax.ppermute(row_far, 'row', far_row)  4.23 us
    ppermute x5, waiting for transfers between devices, swap(): lax.ppermute(col_near, 'col', near_col)  3.02 us
    ppermute x5, starting transfers between devices, swap(): lax.ppermute(row_near, 'row', near_row)  2.23 us
    ppermute x4, waiting for transfers between devices, doubling(): lax.ppermute(value, axis, [(i, i ^ step) for i in range(count)])  2.1 us
  transfers between devices with their start and end apart: 26, of which 12 were waited for; matrix products, arithmetic and copies ran while one was open for 0% of the time, Pallas kernels for 12%

profile of v1, /device:TPU:0, one launch (start us, length us, event | category | flops | bytes accessed | tf_op | source)
XLA Modules:
  0.0 72.8 jit_solution(16274726552410663859)
XLA Ops:
  0.6 0.8 %copy.13.refs_0_ = s32[7,3]{1,0:T(8,128)S(1)} copy(s32[7,3]{0,1:T(4,128)} %param.8) | data formatting | bytes 168 | tf_op args[2]
  1.4 3.3 %shard_map.73 = (f32[2,128,128]{2,1,0:T(8,128)S(1)}, f32[3,1,136,128]{3,2,1,0:T(8,128)S(1)}, f32[3,1,136,128]{3,2,1,0:T(8,128)S(1)}, f32[2,1,136,128]{3,2,1,0:T(...) custom-call(s32[7,3]{1,0:T(8,128)S(1)} %copy.13.refs_0_, f32[7,2,128,128]{3,2,1,0:T(8,128)} %bitcast.59, f32[7,2,128,128]{3,2,1,0:T(8,128)} %bitcast.53), custom_call_target="tpu_custom_call" | custom-call | flops 2000000000 | bytes 6000000 | tf_op jit(solution)/shard_map/pallas_call | solution.py:585
  4.7 2.5 %collective-permute-start.64 = (f32[3,1,136,128]{3,2,1,0:T(8,128)S(1)}, f32[3,1,136,128]{3,2,1,0:T(8,128)S(1)}, u32[]{:S(2)}, u32[]{:S(2)}) collective-permute-start(f32[3,1,136,128]{3,2,1,0:T(8,128)S(1)} %get-tuple-element.146), channel_id=1, source_target_pairs={{0,24},{8,16},{16,8},{24,0},{1,25},{9,17},{17,9},{25,1},{2,26},{10... | collective-permute-start | bytes 626696 | tf_op jit(solution)/shard_map/ppermute | solution.py:614
  7.2 4.5 %collective-permute-start.65 = (f32[2,1,136,128]{3,2,1,0:T(8,128)S(1)}, f32[2,1,136,128]{3,2,1,0:T(8,128)S(1)}, u32[]{:S(2)}, u32[]{:S(2)}) collective-permute-start(f32[2,1,136,128]{3,2,1,0:T(8,128)S(1)} %get-tuple-element.147), channel_id=1, source_target_pairs={{0,7},{1,2},{2,1},{3,4},{4,3},{5,6},{6,5},{7,0},{8,15},{9,10},{10,... | collective-permute-start | bytes 417800 | tf_op jit(solution)/shard_map/ppermute | solution.py:611
  12.8 3.6 %collective-permute-done.65 = f32[2,1,136,128]{3,2,1,0:T(8,128)S(1)} collective-permute-done((f32[2,1,136,128]{3,2,1,0:T(8,128)S(1)}, f32[2,1,136,128]{3,2,1,0:T(8,128)S(1)}, u32[]{:S(2)}, u32[]{:S(2)}) %collective-permute-start.65) | collective-permute-done | bytes 139296 | tf_op jit(solution)/shard_map/ppermute | solution.py:611
  16.4 2.9 %collective-permute-done.66 = f32[2,1,136,128]{3,2,1,0:T(8,128)S(1)} collective-permute-done((f32[2,1,136,128]{3,2,1,0:T(8,128)S(1)}, f32[2,1,136,128]{3,2,1,0:T(8,128)S(1)}, u32[]{:S(2)}, u32[]{:S(2)}) %collective-permute-start.66) | collective-permute-done | bytes 139296 | tf_op jit(solution)/shard_map/ppermute | solution.py:612
  19.3 0.6 copy-done.2
  19.9 52.8 %conditional.1 = (f32[1,1,7,2,128,128]{5,4,3,2,1,0:T(8,128)}, f32[1,1,7,2,128,128]{5,4,3,2,1,0:T(8,128)}, f32[2]{0:T(128)}) conditional(s32[]{:T(128)} %bitcast.30, (f32[1,1,7,2,128,128]{5,4,3,2,1,0:T(8,128)S(1)}, s32[7,3]{1,0:T(8,128)S(1)}, s32[3]{0:T(128)S(1)}, f32[2,128,128]{2,1,0:T(8,128)S(1)}, f32[8,128]{1,0:T(8,128)S(1)}, ...), branch_computations={%region_0.1_spmd, %region_1.2_spmd} | conditional | flops 14000015360 | bytes 77294928 | solution.py:793
  19.9 2.5 %branch_0_fun.6 = (f32[7,2,128,128]{3,2,1,0:T(8,128)S(1)}, f32[2,128,128]{2,1,0:T(8,128)S(1)}, f32[2,1,136,128]{3,2,1,0:T(8,128)S(1)}, f32[2,1,136,128]{3,2,1,0:T(8,128)S(1)}, f32[1,1,136,128]{3,2,1,0:T(8,128)S(1)}) custom-call(s32[7,3]{1,0:T(8,128)S(1)} %get-tuple-element.40.refs_0_, s32[3]{0:T(128)S(1)} %get-tuple-element.41.refs_1_, ...), custom_call_target="tpu_custom_call" | custom-call | flops 2000000000 | bytes 6000000 | tf_op jit(solution)/shard_map/cond/branch_0_fun/pallas_call | solution.py:585
  22.6 1.7 %collective-permute-start.1 = (f32[1,1,136,128]{3,2,1,0:T(8,128)S(1)}, f32[1,1,136,128]{3,2,1,0:T(8,128)S(1)}, u32[]{:S(2)}, u32[]{:S(2)}) collective-permute-start(f32[1,1,136,128]{3,2,1,0:T(8,128)S(1)} %get-tuple-element.53), channel_id=1, source_target_pairs={{0,7},{1,2},{2,1},{3,4},{4,3},{5,6},{6,5},{7,0},{8,15},{9,10},{10,... | collective-permute-start | bytes 208904 | tf_op jit(solution)/shard_map/cond/branch_0_fun/ppermute | solution.py:611
  24.5 5.4 %collective-permute-done.1.refs_6_.refs_19_ = f32[1,1,136,128]{3,2,1,0:T(8,128)S(1)} collective-permute-done((f32[1,1,136,128]{3,2,1,0:T(8,128)S(1)}, f32[1,1,136,128]{3,2,1,0:T(8,128)S(1)}, u32[]{:S(2)}, u32[]{:S(2)}) %collective-permute-start.1) | collective-permute-done | bytes 69664 | tf_op jit(solution)/shard_map/cond/branch_0_fun/ppermute | solution.py:611
  30.1 3.8 %branch_0_fun.7 = (f32[7,2,128,128]{3,2,1,0:T(8,128)S(1)}, f32[2,128,128]{2,1,0:T(8,128)S(1)}, f32[2,128,128]{2,1,0:T(8,128)S(1)}, f32[2,128,128]{2,1,0:T(8,128)...) custom-call(s32[7,3]{1,0:T(8,128)S(1)} %get-tuple-element.40.refs_0_, ...), custom_call_target="tpu_custom_call" | custom-call | flops 2000000000 | bytes 6000000 | tf_op jit(solution)/shard_map/cond/branch_0_fun/pallas_call | solution.py:585
  34.0 1.6 %collective-permute-start.7 = (f32[4,1,136,128]{3,2,1,0:T(8,128)S(1)}, f32[4,1,136,128]{3,2,1,0:T(8,128)S(1)}, u32[]{:S(2)}, u32[]{:S(2)}) collective-permute-start(f32[4,1,136,128]{3,2,1,0:T(8,128)S(1)} %get-tuple-element.57), channel_id=1, source_target_pairs={{0,24},{8,16},{16,8},{24,0},{1,25},{9,17},{17,9},{25,1},{2,26},{10... | collective-permute-start | bytes 835592 | tf_op jit(solution)/shard_map/cond/branch_0_fun/ppermute | solution.py:614
  35.6 3.0 %collective-permute-start.4 = (f32[1,1,136,128]{3,2,1,0:T(8,128)S(1)}, f32[1,1,136,128]{3,2,1,0:T(8,128)S(1)}, u32[]{:S(2)}, u32[]{:S(2)}) collective-permute-start(f32[1,1,136,128]{3,2,1,0:T(8,128)S(1)} %get-tuple-element.55), channel_id=1, source_target_pairs={{0,7},{1,2},{2,1},{3,4},{4,3},{5,6},{6,5},{7,0},{8,15},{9,10},{10,... | collective-permute-start | bytes 208904 | tf_op jit(solution)/shard_map/cond/branch_0_fun/ppermute | solution.py:611
  38.6 0.5 collective-permute-start.8
  39.1 3.3 %collective-permute-done.7.refs_5_.refs_14_.refs_18_ = f32[4,1,136,128]{3,2,1,0:T(8,128)S(1)} collective-permute-done((f32[4,1,136,128]{3,2,1,0:T(8,128)S(1)}, f32[4,1,136,128]{3,2,1,0:T(8,128)S(1)}, u32[]{:S(2)}, u32[]{:S(2)}) %collective-permute-start.7) | collective-permute-done | bytes 278560 | tf_op jit(solution)/shard_map/cond/branch_0_fun/ppermute | solution.py:614
  42.5 0.7 collective-permute-done.8
  43.2 3.4 %branch_0_fun.9 = (f32[7,2,128,128]{3,2,1,0:T(8,128)S(1)}, f32[2,128,128]{2,1,0:T(8,128)S(1)}, f32[8,128]{1,0:T(8,128)S(1)}, f32[2,1,136,128]{3,2,1,0:T(8,128)S(...) custom-call(s32[7,3]{1,0:T(8,128)S(1)} %get-tuple-element.40.refs_0_, ...), custom_call_target="tpu_custom_call" | custom-call | flops 2000000000 | bytes 6000000 | tf_op jit(solution)/shard_map/cond/branch_0_fun/pallas_call | solution.py:585
  47.2 1.5 %collective-permute-start.14 = (f32[1,1,136,128]{3,2,1,0:T(8,128)S(1)}, f32[1,1,136,128]{3,2,1,0:T(8,128)S(1)}, u32[]{:S(2)}, u32[]{:S(2)}) collective-permute-start(f32[1,1,136,128]{3,2,1,0:T(8,128)S(1)} %get-tuple-element.66), channel_id=1, source_target_pairs={{0,1},{1,0},{2,3},{3,2},{4,5},{5,4},{6,7},{7,6},{8,9},{9,8},{10,11... | collective-permute-start | bytes 208904 | tf_op jit(solution)/shard_map/cond/branch_0_fun/ppermute | solution.py:612
  48.7 3.0 %collective-permute-start.13 = (f32[1,1,136,128]{3,2,1,0:T(8,128)S(1)}, f32[1,1,136,128]{3,2,1,0:T(8,128)S(1)}, u32[]{:S(2)}, u32[]{:S(2)}) collective-permute-start(f32[1,1,136,128]{3,2,1,0:T(8,128)S(1)} %get-tuple-element.66), channel_id=1, source_target_pairs={{0,7},{1,2},{2,1},{3,4},{4,3},{5,6},{6,5},{7,0},{8,15},{9,10},{10,... | collective-permute-start | bytes 208904 | tf_op jit(solution)/shard_map/cond/branch_0_fun/ppermute | solution.py:611
  51.8 1.5 %collective-permute-start.15 = (f32[2,1,136,128]{3,2,1,0:T(8,128)S(1)}, f32[2,1,136,128]{3,2,1,0:T(8,128)S(1)}, u32[]{:S(2)}, u32[]{:S(2)}) collective-permute-start(f32[2,1,136,128]{3,2,1,0:T(8,128)S(1)} %get-tuple-element.70), channel_id=1, source_target_pairs={{0,8},{8,0},{16,24},{24,16},{1,9},{9,1},{17,25},{25,17},{2,10},{10... | collective-permute-start | bytes 417800 | tf_op jit(solution)/shard_map/cond/branch_0_fun/ppermute | solution.py:613
  53.4 2.6 %branch_0_fun.8 = (f32[7,2,128,128]{3,2,1,0:T(8,128)}, f32[8,128]{1,0:T(8,128)S(1)}) custom-call(s32[7,3]{1,0:T(8,128)S(1)} %get-tuple-element.40.refs_0_, s32[3]{0:T(128)S(1)} %get-tuple-element.41.refs_1_, f32[1,1,136,128]{3,2,1,0:T(8,128)S(1)} %collective-permute-done.4.refs_2_.refs_11_.refs_15_, ...), custom_call_target="tpu_custom_call" | custom-call | flops 2000000000 | bytes 6000000 | tf_op jit(solution)/shard_map/cond/branch_0_fun/pallas_call | solution.py:585
  56.0 1.9 %collective-permute-done.11 = f32[8,128]{1,0:T(8,128)S(1)} collective-permute-done((f32[8,128]{1,0:T(8,128)S(1)}, f32[8,128]{1,0:T(8,128)S(1)}, u32[]{:S(2)}, u32[]{:S(2)}) %collective-permute-start.11) | collective-permute-done | bytes 4128 | tf_op jit(solution)/shard_map/cond/branch_0_fun/ppermute | solution.py:635
  57.9 3.5 %branch_0_fun.10 = (f32[7,2,128,128]{3,2,1,0:T(8,128)S(1)}, f32[2,128,128]{2,1,0:T(8,128)S(1)}, f32[8,128]{1,0:T(8,128)S(1)}, f32[2,1,136,128]{3,2,1,0:T(8,128)S...) custom-call(s32[7,3]{1,0:T(8,128)S(1)} %get-tuple-element.40.refs_0_, ...), custom_call_target="tpu_custom_call" | custom-call | flops 2000000000 | bytes 6000000 | tf_op jit(solution)/shard_map/cond/branch_0_fun/pallas_call | solution.py:585
  61.5 0.5 collective-permute-start.18
  62.0 3.0 %collective-permute-start.17 = (f32[1,1,136,128]{3,2,1,0:T(8,128)S(1)}, f32[1,1,136,128]{3,2,1,0:T(8,128)S(1)}, u32[]{:S(2)}, u32[]{:S(2)}) collective-permute-start(f32[1,1,136,128]{3,2,1,0:T(8,128)S(1)} %get-tuple-element.74), channel_id=1, source_target_pairs={{0,7},{1,2},{2,1},{3,4},{4,3},{5,6},{6,5},{7,0},{8,15},{9,10},{10,... | collective-permute-start | bytes 208904 | tf_op jit(solution)/shard_map/cond/branch_0_fun/ppermute | solution.py:611
  64.9 1.5 %collective-permute-start.20 = (f32[8,128]{1,0:T(8,128)S(1)}, f32[8,128]{1,0:T(8,128)S(1)}, u32[]{:S(2)}, u32[]{:S(2)}) collective-permute-start(f32[8,128]{1,0:T(8,128)S(1)} %get-tuple-element.76), channel_id=1, source_target_pairs={{0,16},{8,24},{16,0},{24,8},{1,17},{9,25},{17,1},{25,9},{2,18},{10... | collective-permute-start | bytes 12296 | tf_op jit(solution)/shard_map/cond/branch_0_fun/ppermute | solution.py:655
  66.4 0.9 %collective-permute-done.16.refs_9_ = f32[2,1,136,128]{3,2,1,0:T(8,128)S(1)} collective-permute-done((f32[2,1,136,128]{3,2,1,0:T(8,128)S(1)}, f32[2,1,136,128]{3,2,1,0:T(8,128)S(1)}, u32[]{:S(2)}, u32[]{:S(2)}) %collective-permute-start.16) | collective-permute-done | bytes 139296 | tf_op jit(solution)/shard_map/cond/branch_0_fun/ppermute | solution.py:614
  67.8 0.8 %collective-permute-done.20 = f32[8,128]{1,0:T(8,128)S(1)} collective-permute-done((f32[8,128]{1,0:T(8,128)S(1)}, f32[8,128]{1,0:T(8,128)S(1)}, u32[]{:S(2)}, u32[]{:S(2)}) %collective-permute-start.20) | collective-permute-done | bytes 4128 | tf_op jit(solution)/shard_map/cond/branch_0_fun/ppermute | solution.py:655
  68.6 0.5 collective-permute-done.17.refs_6_
  69.0 3.1 %branch_0_fun.11 = f32[7,2,128,128]{3,2,1,0:T(8,128)} custom-call(s32[7,3]{1,0:T(8,128)S(1)} %get-tuple-element.40.refs_0_, s32[3]{0:T(128)S(1)} %get-tuple-element.41.refs_1_, f32[7,2,128,128]{3,2,1,0:T(8,128)S(1)} %get-tuple-element.71.refs_2_, f32[7,2,128,128]{3,2,1,0:T(8,128)S(1)} %bitcast.62, f32[2,128,128]{2,1,0:T(8,128)S(1)} %get-tuple-element.72.refs_4_, ...), custom_call_target="tpu_custom_call" | custom-call | flops 2000000000 | bytes 6000000 | tf_op jit(solution)/shard_map/cond/branch_0_fun/pallas_call | solution.py:585
  72.2 0.5 fusion.4
  (52 shorter events, 2.6 us)
Async XLA Ops:
  1.4 17.8 %copy-start = (f32[1,1,7,2,128,128]{5,4,3,2,1,0:T(8,128)S(1)}, f32[1,1,7,2,128,128]{5,4,3,2,1,0:T(8,128)}, u32[]{:S(2)}) copy-start(f32[1,1,7,2,128,128]{5,4,3,2,1,0:T(8,128)} %param.7) | copy-start | bytes 2752516
  1.4 17.9 %copy-start.1 = (f32[1,1,7,2,128,128]{5,4,3,2,1,0:T(8,128)S(1)}, f32[1,1,7,2,128,128]{5,4,3,2,1,0:T(8,128)}, u32[]{:S(2)}) copy-start(f32[1,1,7,2,128,128]{5,4,3,2,1,0:T(8,128)} %param.6) | copy-start | bytes 2752516
  4.7 11.6 %collective-permute-start.64 = (f32[3,1,136,128]{3,2,1,0:T(8,128)S(1)}, f32[3,1,136,128]{3,2,1,0:T(8,128)S(1)}, u32[]{:S(2)}, u32[]{:S(2)}) collective-permute-start(f32[3,1,136,128]{3,2,1,0:T(8,128)S(1)} %get-tuple-element.146), channel_id=1, source_target_pairs={{0,24},{8,16},{16,8},{24,0},{1,25},{9,17},{17,9},{25,1},{2,26},{10... | collective-permute-start | bytes 626696 | tf_op jit(solution)/shard_map/ppermute | solution.py:614
  7.2 9.1 %collective-permute-start.65 = (f32[2,1,136,128]{3,2,1,0:T(8,128)S(1)}, f32[2,1,136,128]{3,2,1,0:T(8,128)S(1)}, u32[]{:S(2)}, u32[]{:S(2)}) collective-permute-start(f32[2,1,136,128]{3,2,1,0:T(8,128)S(1)} %get-tuple-element.147), channel_id=1, source_target_pairs={{0,7},{1,2},{2,1},{3,4},{4,3},{5,6},{6,5},{7,0},{8,15},{9,10},{10,... | collective-permute-start | bytes 417800 | tf_op jit(solution)/shard_map/ppermute | solution.py:611
  11.7 7.5 %collective-permute-start.66 = (f32[2,1,136,128]{3,2,1,0:T(8,128)S(1)}, f32[2,1,136,128]{3,2,1,0:T(8,128)S(1)}, u32[]{:S(2)}, u32[]{:S(2)}) collective-permute-start(f32[2,1,136,128]{3,2,1,0:T(8,128)S(1)} %get-tuple-element.147), channel_id=1, source_target_pairs={{0,1},{1,0},{2,3},{3,2},{4,5},{5,4},{6,7},{7,6},{8,9},{9,8},{10,11... | collective-permute-start | bytes 417800 | tf_op jit(solution)/shard_map/ppermute | solution.py:612
  11.7 7.5 %collective-permute-start.67 = (f32[3,1,136,128]{3,2,1,0:T(8,128)S(1)}, f32[3,1,136,128]{3,2,1,0:T(8,128)S(1)}, u32[]{:S(2)}, u32[]{:S(2)}) collective-permute-start(f32[3,1,136,128]{3,2,1,0:T(8,128)S(1)} %get-tuple-element.148), channel_id=1, source_target_pairs={{0,8},{8,0},{16,24},{24,16},{1,9},{9,1},{17,25},{25,17},{2,10},{10... | collective-permute-start | bytes 626696 | tf_op jit(solution)/shard_map/ppermute | solution.py:613
  19.2 0.7 copy-start.2
  22.4 7.6 %collective-permute-start = (f32[2,1,136,128]{3,2,1,0:T(8,128)S(1)}, f32[2,1,136,128]{3,2,1,0:T(8,128)S(1)}, u32[]{:S(2)}, u32[]{:S(2)}) collective-permute-start(f32[2,1,136,128]{3,2,1,0:T(8,128)S(1)} %get-tuple-element.52), channel_id=1, source_target_pairs={{0,24},{8,16},{16,8},{24,0},{1,25},{9,17},{17,9},{25,1},{2,26},{10... | collective-permute-start | bytes 417800 | tf_op jit(solution)/shard_map/cond/branch_0_fun/ppermute | solution.py:614
  22.6 7.4 %collective-permute-start.1 = (f32[1,1,136,128]{3,2,1,0:T(8,128)S(1)}, f32[1,1,136,128]{3,2,1,0:T(8,128)S(1)}, u32[]{:S(2)}, u32[]{:S(2)}) collective-permute-start(f32[1,1,136,128]{3,2,1,0:T(8,128)S(1)} %get-tuple-element.53), channel_id=1, source_target_pairs={{0,7},{1,2},{2,1},{3,4},{4,3},{5,6},{6,5},{7,0},{8,15},{9,10},{10,... | collective-permute-start | bytes 208904 | tf_op jit(solution)/shard_map/cond/branch_0_fun/ppermute | solution.py:611
  24.3 5.8 %collective-permute-start.2 = (f32[1,1,136,128]{3,2,1,0:T(8,128)S(1)}, f32[1,1,136,128]{3,2,1,0:T(8,128)S(1)}, u32[]{:S(2)}, u32[]{:S(2)}) collective-permute-start(f32[1,1,136,128]{3,2,1,0:T(8,128)S(1)} %get-tuple-element.53), channel_id=1, source_target_pairs={{0,1},{1,0},{2,3},{3,2},{4,5},{5,4},{6,7},{7,6},{8,9},{9,8},{10,11... | collective-permute-start | bytes 208904 | tf_op jit(solution)/shard_map/cond/branch_0_fun/ppermute | solution.py:612
  24.3 5.8 %collective-permute-start.3 = (f32[2,1,136,128]{3,2,1,0:T(8,128)S(1)}, f32[2,1,136,128]{3,2,1,0:T(8,128)S(1)}, u32[]{:S(2)}, u32[]{:S(2)}) collective-permute-start(f32[2,1,136,128]{3,2,1,0:T(8,128)S(1)} %get-tuple-element.54), channel_id=1, source_target_pairs={{0,8},{8,0},{16,24},{24,16},{1,9},{9,1},{17,25},{25,17},{2,10},{10... | collective-permute-start | bytes 417800 | tf_op jit(solution)/shard_map/cond/branch_0_fun/ppermute | solution.py:613
  33.9 5.2 %collective-permute-start.6 = (f32[4,1,136,128]{3,2,1,0:T(8,128)S(1)}, f32[4,1,136,128]{3,2,1,0:T(8,128)S(1)}, u32[]{:S(2)}, u32[]{:S(2)}) collective-permute-start(f32[4,1,136,128]{3,2,1,0:T(8,128)S(1)} %get-tuple-element.56), channel_id=1, source_target_pairs={{0,8},{8,0},{16,24},{24,16},{1,9},{9,1},{17,25},{25,17},{2,10},{10... | collective-permute-start | bytes 835592 | tf_op jit(solution)/shard_map/cond/branch_0_fun/ppermute | solution.py:613
  34.0 8.5 %collective-permute-start.7 = (f32[4,1,136,128]{3,2,1,0:T(8,128)S(1)}, f32[4,1,136,128]{3,2,1,0:T(8,128)S(1)}, u32[]{:S(2)}, u32[]{:S(2)}) collective-permute-start(f32[4,1,136,128]{3,2,1,0:T(8,128)S(1)} %get-tuple-element.57), channel_id=1, source_target_pairs={{0,24},{8,16},{16,8},{24,0},{1,25},{9,17},{17,9},{25,1},{2,26},{10... | collective-permute-start | bytes 835592 | tf_op jit(solution)/shard_map/cond/branch_0_fun/ppermute | solution.py:614
  35.6 7.5 %collective-permute-start.5 = (f32[1,1,136,128]{3,2,1,0:T(8,128)S(1)}, f32[1,1,136,128]{3,2,1,0:T(8,128)S(1)}, u32[]{:S(2)}, u32[]{:S(2)}) collective-permute-start(f32[1,1,136,128]{3,2,1,0:T(8,128)S(1)} %get-tuple-element.55), channel_id=1, source_target_pairs={{0,1},{1,0},{2,3},{3,2},{4,5},{5,4},{6,7},{7,6},{8,9},{9,8},{10,11... | collective-permute-start | bytes 208904 | tf_op jit(solution)/shard_map/cond/branch_0_fun/ppermute | solution.py:612
  35.6 7.5 %collective-permute-start.4 = (f32[1,1,136,128]{3,2,1,0:T(8,128)S(1)}, f32[1,1,136,128]{3,2,1,0:T(8,128)S(1)}, u32[]{:S(2)}, u32[]{:S(2)}) collective-permute-start(f32[1,1,136,128]{3,2,1,0:T(8,128)S(1)} %get-tuple-element.55), channel_id=1, source_target_pairs={{0,7},{1,2},{2,1},{3,4},{4,3},{5,6},{6,5},{7,0},{8,15},{9,10},{10,... | collective-permute-start | bytes 208904 | tf_op jit(solution)/shard_map/cond/branch_0_fun/ppermute | solution.py:611
  38.6 4.5 %collective-permute-start.8 = (f32[8,128]{1,0:T(8,128)S(1)}, f32[8,128]{1,0:T(8,128)S(1)}, u32[]{:S(2)}, u32[]{:S(2)}) collective-permute-start(f32[8,128]{1,0:T(8,128)S(1)} %get-tuple-element.61), channel_id=1, source_target_pairs={{0,16},{8,24},{16,0},{24,8},{1,17},{9,25},{17,1},{25,9},{2,18},{10... | collective-permute-start | bytes 12296 | tf_op jit(solution)/shard_map/cond/branch_0_fun/ppermute | solution.py:655
  43.1 3.6 %collective-permute-start.9 = (f32[8,128]{1,0:T(8,128)S(1)}, f32[8,128]{1,0:T(8,128)S(1)}, u32[]{:S(2)}, u32[]{:S(2)}) collective-permute-start(f32[8,128]{1,0:T(8,128)S(1)} %add_add_fusion.1), channel_id=1, source_target_pairs={{0,1},{1,0},{2,3},{3,2},{4,5},{5,4},{6,7},{7,6},{8,9},{9,8},{10,11... | collective-permute-start | bytes 12296 | tf_op jit(solution)/shard_map/cond/branch_0_fun/ppermute | solution.py:635
  46.8 6.5 %collective-permute-start.10 = (f32[8,128]{1,0:T(8,128)S(1)}, f32[8,128]{1,0:T(8,128)S(1)}, u32[]{:S(2)}, u32[]{:S(2)}) collective-permute-start(f32[8,128]{1,0:T(8,128)S(1)} %add_select_fusion), channel_id=1, source_target_pairs={{0,2},{1,3},{2,0},{3,1},{4,6},{5,7},{6,4},{7,5},{8,10},{9,11},{10,... | collective-permute-start | bytes 12296 | tf_op jit(solution)/shard_map/cond/branch_0_fun/ppermute | solution.py:635
  47.2 10.6 %collective-permute-start.14 = (f32[1,1,136,128]{3,2,1,0:T(8,128)S(1)}, f32[1,1,136,128]{3,2,1,0:T(8,128)S(1)}, u32[]{:S(2)}, u32[]{:S(2)}) collective-permute-start(f32[1,1,136,128]{3,2,1,0:T(8,128)S(1)} %get-tuple-element.66), channel_id=1, source_target_pairs={{0,1},{1,0},{2,3},{3,2},{4,5},{5,4},{6,7},{7,6},{8,9},{9,8},{10,11... | collective-permute-start | bytes 208904 | tf_op jit(solution)/shard_map/cond/branch_0_fun/ppermute | solution.py:612
  48.7 9.1 %collective-permute-start.13 = (f32[1,1,136,128]{3,2,1,0:T(8,128)S(1)}, f32[1,1,136,128]{3,2,1,0:T(8,128)S(1)}, u32[]{:S(2)}, u32[]{:S(2)}) collective-permute-start(f32[1,1,136,128]{3,2,1,0:T(8,128)S(1)} %get-tuple-element.66), channel_id=1, source_target_pairs={{0,7},{1,2},{2,1},{3,4},{4,3},{5,6},{6,5},{7,0},{8,15},{9,10},{10,... | collective-permute-start | bytes 208904 | tf_op jit(solution)/shard_map/cond/branch_0_fun/ppermute | solution.py:611
  51.7 6.2 %collective-permute-start.12 = (f32[2,1,136,128]{3,2,1,0:T(8,128)S(1)}, f32[2,1,136,128]{3,2,1,0:T(8,128)S(1)}, u32[]{:S(2)}, u32[]{:S(2)}) collective-permute-start(f32[2,1,136,128]{3,2,1,0:T(8,128)S(1)} %get-tuple-element.65), channel_id=1, source_target_pairs={{0,24},{8,16},{16,8},{24,0},{1,25},{9,17},{17,9},{25,1},{2,26},{10... | collective-permute-start | bytes 417800 | tf_op jit(solution)/shard_map/cond/branch_0_fun/ppermute | solution.py:614
  51.8 6.0 %collective-permute-start.15 = (f32[2,1,136,128]{3,2,1,0:T(8,128)S(1)}, f32[2,1,136,128]{3,2,1,0:T(8,128)S(1)}, u32[]{:S(2)}, u32[]{:S(2)}) collective-permute-start(f32[2,1,136,128]{3,2,1,0:T(8,128)S(1)} %get-tuple-element.70), channel_id=1, source_target_pairs={{0,8},{8,0},{16,24},{24,16},{1,9},{9,1},{17,25},{25,17},{2,10},{10... | collective-permute-start | bytes 417800 | tf_op jit(solution)/shard_map/cond/branch_0_fun/ppermute | solution.py:613
  53.3 4.5 %collective-permute-start.11 = (f32[8,128]{1,0:T(8,128)S(1)}, f32[8,128]{1,0:T(8,128)S(1)}, u32[]{:S(2)}, u32[]{:S(2)}) collective-permute-start(f32[8,128]{1,0:T(8,128)S(1)} %add.120), channel_id=1, source_target_pairs={{0,4},{1,5},{2,6},{3,7},{4,0},{5,1},{6,2},{7,3},{8,12},{9,13},{10,... | collective-permute-start | bytes 12296 | tf_op jit(solution)/shard_map/cond/branch_0_fun/ppermute | solution.py:635
  61.4 5.9 %collective-permute-start.16 = (f32[2,1,136,128]{3,2,1,0:T(8,128)S(1)}, f32[2,1,136,128]{3,2,1,0:T(8,128)S(1)}, u32[]{:S(2)}, u32[]{:S(2)}) collective-permute-start(f32[2,1,136,128]{3,2,1,0:T(8,128)S(1)} %get-tuple-element.73), channel_id=1, source_target_pairs={{0,24},{8,16},{16,8},{24,0},{1,25},{9,17},{17,9},{25,1},{2,26},{10... | collective-permute-start | bytes 417800 | tf_op jit(solution)/shard_map/cond/branch_0_fun/ppermute | solution.py:614
  61.5 7.6 %collective-permute-start.18 = (f32[1,1,136,128]{3,2,1,0:T(8,128)S(1)}, f32[1,1,136,128]{3,2,1,0:T(8,128)S(1)}, u32[]{:S(2)}, u32[]{:S(2)}) collective-permute-start(f32[1,1,136,128]{3,2,1,0:T(8,128)S(1)} %get-tuple-element.74), channel_id=1, source_target_pairs={{0,1},{1,0},{2,3},{3,2},{4,5},{5,4},{6,7},{7,6},{8,9},{9,8},{10,11... | collective-permute-start | bytes 208904 | tf_op jit(solution)/shard_map/cond/branch_0_fun/ppermute | solution.py:612
  62.0 7.0 %collective-permute-start.17 = (f32[1,1,136,128]{3,2,1,0:T(8,128)S(1)}, f32[1,1,136,128]{3,2,1,0:T(8,128)S(1)}, u32[]{:S(2)}, u32[]{:S(2)}) collective-permute-start(f32[1,1,136,128]{3,2,1,0:T(8,128)S(1)} %get-tuple-element.74), channel_id=1, source_target_pairs={{0,7},{1,2},{2,1},{3,4},{4,3},{5,6},{6,5},{7,0},{8,15},{9,10},{10,... | collective-permute-start | bytes 208904 | tf_op jit(solution)/shard_map/cond/branch_0_fun/ppermute | solution.py:611
  64.9 3.6 %collective-permute-start.20 = (f32[8,128]{1,0:T(8,128)S(1)}, f32[8,128]{1,0:T(8,128)S(1)}, u32[]{:S(2)}, u32[]{:S(2)}) collective-permute-start(f32[8,128]{1,0:T(8,128)S(1)} %get-tuple-element.76), channel_id=1, source_target_pairs={{0,16},{8,24},{16,0},{24,8},{1,17},{9,25},{17,1},{25,9},{2,18},{10... | collective-permute-start | bytes 12296 | tf_op jit(solution)/shard_map/cond/branch_0_fun/ppermute | solution.py:655
  66.4 1.4 %collective-permute-start.19 = (f32[2,1,136,128]{3,2,1,0:T(8,128)S(1)}, f32[2,1,136,128]{3,2,1,0:T(8,128)S(1)}, u32[]{:S(2)}, u32[]{:S(2)}) collective-permute-start(f32[2,1,136,128]{3,2,1,0:T(8,128)S(1)} %get-tuple-element.75), channel_id=1, source_target_pairs={{0,8},{8,0},{16,24},{24,16},{1,9},{9,1},{17,25},{25,17},{2,10},{10... | collective-permute-start | bytes 417800 | tf_op jit(solution)/shard_map/cond/branch_0_fun/ppermute | solution.py:613
  68.6 3.6 %collective-permute-start.21 = (f32[8,128]{1,0:T(8,128)S(1)}, f32[8,128]{1,0:T(8,128)S(1)}, u32[]{:S(2)}, u32[]{:S(2)}) collective-permute-start(f32[8,128]{1,0:T(8,128)S(1)} %add_add_fusion), channel_id=1, source_target_pairs={{0,1},{1,0},{2,3},{3,2},{4,5},{5,4},{6,7},{7,6},{8,9},{9,8},{10,11... | collective-permute-start | bytes 12296 | tf_op jit(solution)/shard_map/cond/branch_0_fun/ppermute | solution.py:635

commit v2 on v1

--- a/solution.py
+++ b/solution.py
@@ -10,7 +10,7 @@
 F32 = jnp.float32
 BF16 = jnp.bfloat16
 EXTRA = 8
-SIDES = ("col_far", "col_near", "row_near", "row_far")
+SIDES = ("row_far", "col_far", "col_near", "row_near")
 
 
 def each(count, body, rolled):
@@ -23,7 +23,7 @@
         body(i)
         return carry
 
-    lax.fori_loop(0, count, step, 0)
+    lax.fori_loop(0, count, step, 0, unroll=2)
 
 
 def total_of(count, term, first, rolled):
@@ -410,11 +410,8 @@
     split_all(k.h, k.hs, closed)
     vertex_sums(k.off, k.hs, k.ns, k.acc_h, closed)
     send_sums(k.acc_h, 2, k.near, k.far, True)
-    vertex_sums(k.off, k.ns, k.xs, k.acc_cross, closed)
-    send_sums(k.acc_cross, 3, k.near, k.far, True)
     for s in range(layers):
         k.h_local[s] = symmetric(k.acc_h[1, s])
-        k.cross_local[s] = symmetric(k.acc_cross[1, s])
     if closed:
         closed_send(k, "out", None, k.hs, k.ns, True, 2, None)
         closed_send(k, "out", None, k.ns, k.xs, True, 3, None)
@@ -432,6 +429,15 @@
     part = (1.0 + s_next) * trace - s_next * squares
     k.sums[...] = jnp.broadcast_to(jnp.sum(part, keepdims=True), k.sums.shape)
     put_row((k.near, k.far, k.side), k.sums[0:1, :])
+
+
+def cross_kernel(closed, k):
+    split_all(k.x, k.xs, closed)
+    split_all(k.before, k.bs, closed)
+    vertex_sums(k.off, k.xs, k.bs, k.acc, closed)
+    send_sums(k.acc, 0, k.near, k.far, True)
+    for s in range(k.x.shape[1]):
+        k.local[s] = symmetric(k.acc[1, s])
 
 
 def last_square_kernel(step, sums_at, closed, k):
@@ -503,6 +509,9 @@
 
     energy = total_of(k.x.shape[0] * layers, weigh, jnp.zeros_like(k.x[0, 0]), closed)
     k.energy[...] = jnp.broadcast_to(0.5 * jnp.sum(energy, keepdims=True), k.energy.shape)
+    for ref, cross in ((k.near, k.cross_near), (k.far, k.cross_far)):
+        for pair in range(layers // 2):
+            ref[2, pair] = cross[0, pair]
 
 
 def next_gradient_kernel(step, order, closed, k):
@@ -538,7 +547,7 @@
     fill_neighbours(k.g_cols, own_g, both["col_near"], both["col_far"], odd("col"), blocks)
     diagonal_blocks(k, "m", own_x, k.x_rows, k.x_cols, 0)
     own_sums = add_sums([k.g_local[s] for s in range(layers)], k.gm_row_near, k.gm_row_far, 1)
-    cross_sums = add_sums([k.cross_local[s] for s in range(layers)], k.am_row_near, k.am_row_far, 3)
+    cross_sums = add_sums([k.cross_local[s] for s in range(layers)], k.gm_row_near, k.gm_row_far, 2)
     twice = 2.0 * (1.0 + s_after) * excess
     for s in range(layers):
         cross = own_sums[s] + scale * cross_sums[s] + twice * own_x[s]
@@ -727,21 +736,24 @@
     k = call(
         lambda k: turn_square_kernel(1, 1, closed, k), smem,
         dict(x=x1, x_local=local1, h=h, first=near1["first"], **named("m", near1), **edges(e=edge1)),
-        dict(new=full, local=local, h_local=local, cross_local=local, sums=tile,
-             **shape.messages(4, 1), **shape.edges(4, closed)),
-        dict(ns=split, hs=split, acc=acc, acc_h=acc, acc_cross=acc, **square_scratch),
-    )
-    x2, local2, h_local, cross_local, occupied, near2 = (
-        k.new, k.local, k.h_local, k.cross_local, k.sums, exchange(k)
-    )
+        dict(new=full, local=local, h_local=local, sums=tile,
+             **shape.messages(3, 1), **shape.edges(4, closed)),
+        dict(ns=split, hs=split, acc=acc, acc_h=acc, **square_scratch),
+    )
+    x2, local2, h_local, occupied, near2 = k.new, k.local, k.h_local, k.sums, exchange(k)
     if closed:
         edge2 = exchange_edges(k)
+    cross = call(
+        lambda k: cross_kernel(closed, k), dict(off=table), dict(x=x2, before=x1),
+        dict(near=(1, *shape.pairs), far=(1, *shape.pairs), local=local), dict(xs=split, bs=split, acc=acc),
+    )
     occupied = col_first(row_total(occupied, near2))
     k = call(
         lambda k: first_gradient_kernel(2, closed, k), smem,
-        dict(h=h, x=x2, before=x1, h_local=h_local, first=near2["first"], **named("h", near0), **named("m", near2),
+        dict(h=h, x=x2, before=x1, h_local=h_local, first=near2["first"],
+             cross_near=cross.near, cross_far=cross.far, **named("h", near0), **named("m", near2),
              **edges(he=edge0, e=edge2)),
-        dict(new=full, local=local, energy=tile, **shape.messages(2, 1), **shape.edges(2, closed)),
+        dict(new=full, local=local, energy=tile, **shape.messages(3, 1), **shape.edges(2, closed)),
         dict(**pair_scratch, **tail),
     )
     gh, gh_local, energy, near_gh = k.new, k.local, k.energy, exchange(k)
@@ -758,7 +770,7 @@
     k = call(
         lambda k: next_gradient_kernel(1, order, closed, k), smem,
         dict(sums=sums, done=done, first=near_gh["first"], gh=gh, after=x2, x=x1, before=x0, g_local=gh_local,
-             cross_local=cross_local, **named("gm", near_gh), **named("am", near2), **named("m", near1),
+             cross_local=cross.local, **named("gm", near_gh), **named("am", near2), **named("m", near1),
              **edges(ge=edge_gh, ae=edge2, e=edge1)),
         dict(new=full, local=local, energy=tile,
              **shape.messages(2, 1), **shape.edges(2, closed)),

time: 73 us -> 70.9 us (0.971)
  waiting for transfers between devices: 20.7 us -> 18.5 us
  starting transfers between devices: 26.4 us -> 25.1 us
  Pallas kernels: 22.2 us -> 23.4 us
    ppermute x5, waiting for transfers between devices: 4.23 us -> 1.95 us  [swap(): lax.ppermute(row_far, 'row', far_row)]
    ppermute x5, starting transfers between devices: 2.23 us -> 0.82 us  [swap(): lax.ppermute(row_near, 'row', near_row)]
    pallas_call x7 -> x8, Pallas kernels: 22.2 us -> 23.4 us  [call(): pl.pallas_call(body, out_shape=[jax.ShapeDtypeStruct(shape, F32) for shap...]
    ppermute x5, starting transfers between devices: 15.1 us -> 16.3 us  [swap(): lax.ppermute(col_far, 'col', far_col)]
    ppermute x5, starting transfers between devices: 4.52 us -> 3.71 us  [swap(): lax.ppermute(row_far, 'row', far_row)]
  transfers between devices with their start and end apart: 26 -> 26, of which waited for: 12 -> 12; matrix products, arithmetic and copies ran while one was open for 0% -> 0% of each run, Pallas kernels for 12% -> 15%
where the time goes in v2:
time: 70.9 us; the launch traced here: 70.7 us
  starting transfers between devices  25.1 us (35%)
  Pallas kernels  23.4 us (33%)
  waiting for transfers between devices  18.5 us (26%)
  between operations  1.53 us (2%)
  local copies, waits for them, and re-layouts  1.43 us (2%)
    pallas_call x8, Pallas kernels, call(): pl.pallas_call(body, out_shape=[jax.ShapeDtypeStruct(shape, F32) for shap...  23.4 us
    ppermute x5, starting transfers between devices, swap(): lax.ppermute(col_far, 'col', far_col)  16.3 us
    ppermute x5, waiting for transfers between devices, swap(): lax.ppermute(col_far, 'col', far_col)  10.1 us
    ppermute x5, starting transfers between devices, swap(): lax.ppermute(row_far, 'row', far_row)  3.71 us
    ppermute x5, waiting for transfers between devices, swap(): lax.ppermute(col_near, 'col', near_col)  3.03 us
    ppermute x5, waiting for transfers between devices, swap(): lax.ppermute(row_far, 'row', far_row)  1.95 us
    ppermute x2, starting transfers between devices, row_total(): rest = lax.ppermute(value, 'row', [(i, i ^ 2) for i in range(4)])  1.79 us
    ppermute x5, starting transfers between devices, swap(): lax.ppermute(col_near, 'col', near_col)  1.58 us
  transfers between devices with their start and end apart: 26, of which 12 were waited for; matrix products, arithmetic and copies ran while one was open for 0% of the time, Pallas kernels for 15%

profile of v2, /device:TPU:0, one launch (start us, length us, event | category | flops | bytes accessed | tf_op | source)
XLA Modules:
  0.0 70.7 jit_solution(6330802900325588956)
XLA Ops:
  0.6 0.8 %copy.13.refs_0_ = s32[7,3]{1,0:T(8,128)S(1)} copy(s32[7,3]{0,1:T(4,128)} %param.8) | data formatting | bytes 168 | tf_op args[2]
  1.4 3.3 %shard_map.73 = (f32[2,128,128]{2,1,0:T(8,128)S(1)}, f32[3,1,136,128]{3,2,1,0:T(8,128)S(1)}, f32[3,1,136,128]{3,2,1,0:T(8,128)S(1)}, f32[2,1,136,128]{3,2,1,0:T(...) custom-call(s32[7,3]{1,0:T(8,128)S(1)} %copy.13.refs_0_, f32[7,2,128,128]{3,2,1,0:T(8,128)} %bitcast.59, f32[7,2,128,128]{3,2,1,0:T(8,128)} %bitcast.53), custom_call_target="tpu_custom_call" | custom-call | flops 2000000000 | bytes 6000000 | tf_op jit(solution)/shard_map/pallas_call | solution.py:594
  4.7 2.5 %collective-permute-start.64 = (f32[3,1,136,128]{3,2,1,0:T(8,128)S(1)}, f32[3,1,136,128]{3,2,1,0:T(8,128)S(1)}, u32[]{:S(2)}, u32[]{:S(2)}) collective-permute-start(f32[3,1,136,128]{3,2,1,0:T(8,128)S(1)} %get-tuple-element.150), channel_id=1, source_target_pairs={{0,24},{8,16},{16,8},{24,0},{1,25},{9,17},{17,9},{25,1},{2,26},{10... | collective-permute-start | bytes 626696 | tf_op jit(solution)/shard_map/ppermute | solution.py:623
  7.2 4.5 %collective-permute-start.65 = (f32[2,1,136,128]{3,2,1,0:T(8,128)S(1)}, f32[2,1,136,128]{3,2,1,0:T(8,128)S(1)}, u32[]{:S(2)}, u32[]{:S(2)}) collective-permute-start(f32[2,1,136,128]{3,2,1,0:T(8,128)S(1)} %get-tuple-element.151), channel_id=1, source_target_pairs={{0,7},{1,2},{2,1},{3,4},{4,3},{5,6},{6,5},{7,0},{8,15},{9,10},{10,... | collective-permute-start | bytes 417800 | tf_op jit(solution)/shard_map/ppermute | solution.py:620
  12.8 3.6 %collective-permute-done.65 = f32[2,1,136,128]{3,2,1,0:T(8,128)S(1)} collective-permute-done((f32[2,1,136,128]{3,2,1,0:T(8,128)S(1)}, f32[2,1,136,128]{3,2,1,0:T(8,128)S(1)}, u32[]{:S(2)}, u32[]{:S(2)}) %collective-permute-start.65) | collective-permute-done | bytes 139296 | tf_op jit(solution)/shard_map/ppermute | solution.py:620
  16.4 2.9 %collective-permute-done.66 = f32[2,1,136,128]{3,2,1,0:T(8,128)S(1)} collective-permute-done((f32[2,1,136,128]{3,2,1,0:T(8,128)S(1)}, f32[2,1,136,128]{3,2,1,0:T(8,128)S(1)}, u32[]{:S(2)}, u32[]{:S(2)}) %collective-permute-start.66) | collective-permute-done | bytes 139296 | tf_op jit(solution)/shard_map/ppermute | solution.py:621
  19.3 0.6 copy-done.2
  19.9 50.6 %conditional.1 = (f32[1,1,7,2,128,128]{5,4,3,2,1,0:T(8,128)}, f32[1,1,7,2,128,128]{5,4,3,2,1,0:T(8,128)}, f32[2]{0:T(128)}) conditional(s32[]{:T(128)} %bitcast.30, (f32[1,1,7,2,128,128]{5,4,3,2,1,0:T(8,128)S(1)}, s32[7,3]{1,0:T(8,128)S(1)}, s32[3]{0:T(128)S(1)}, f32[2,128,128]{2,1,0:T(8,128)S(1)}, f32[8,128]{1,0:T(8,128)S(1)}, ...), branch_computations={%region_0.1_spmd, %region_1.2_spmd} | conditional | flops 16000015360 | bytes 83294928 | solution.py:805
  19.9 2.5 %branch_0_fun.7 = (f32[7,2,128,128]{3,2,1,0:T(8,128)S(1)}, f32[2,128,128]{2,1,0:T(8,128)S(1)}, f32[2,1,136,128]{3,2,1,0:T(8,128)S(1)}, f32[2,1,136,128]{3,2,1,0:T(8,128)S(1)}, f32[1,1,136,128]{3,2,1,0:T(8,128)S(1)}) custom-call(s32[7,3]{1,0:T(8,128)S(1)} %get-tuple-element.40.refs_0_, s32[3]{0:T(128)S(1)} %get-tuple-element.41.refs_1_, ...), custom_call_target="tpu_custom_call" | custom-call | flops 2000000000 | bytes 6000000 | tf_op jit(solution)/shard_map/cond/branch_0_fun/pallas_call | solution.py:594
  22.6 1.7 %collective-permute-start.1 = (f32[1,1,136,128]{3,2,1,0:T(8,128)S(1)}, f32[1,1,136,128]{3,2,1,0:T(8,128)S(1)}, u32[]{:S(2)}, u32[]{:S(2)}) collective-permute-start(f32[1,1,136,128]{3,2,1,0:T(8,128)S(1)} %get-tuple-element.53), channel_id=1, source_target_pairs={{0,7},{1,2},{2,1},{3,4},{4,3},{5,6},{6,5},{7,0},{8,15},{9,10},{10,... | collective-permute-start | bytes 208904 | tf_op jit(solution)/shard_map/cond/branch_0_fun/ppermute | solution.py:620
  24.5 5.4 %collective-permute-done.1.refs_7_.refs_20_ = f32[1,1,136,128]{3,2,1,0:T(8,128)S(1)} collective-permute-done((f32[1,1,136,128]{3,2,1,0:T(8,128)S(1)}, f32[1,1,136,128]{3,2,1,0:T(8,128)S(1)}, u32[]{:S(2)}, u32[]{:S(2)}) %collective-permute-start.1) | collective-permute-done | bytes 69664 | tf_op jit(solution)/shard_map/cond/branch_0_fun/ppermute | solution.py:620
  30.1 3.2 %branch_0_fun.8 = (f32[7,2,128,128]{3,2,1,0:T(8,128)S(1)}, f32[2,128,128]{2,1,0:T(8,128)S(1)}, f32[2,128,128]{2,1,0:T(8,128)S(1)}, f32[8,128]{1,0:T(8,128)S(1)},...) custom-call(s32[7,3]{1,0:T(8,128)S(1)} %get-tuple-element.40.refs_0_, ...), custom_call_target="tpu_custom_call" | custom-call | flops 2000000000 | bytes 6000000 | tf_op jit(solution)/shard_map/cond/branch_0_fun/pallas_call | solution.py:594
  33.4 0.6 collective-permute-start.4
  34.0 3.6 %collective-permute-start.5 = (f32[1,1,136,128]{3,2,1,0:T(8,128)S(1)}, f32[1,1,136,128]{3,2,1,0:T(8,128)S(1)}, u32[]{:S(2)}, u32[]{:S(2)}) collective-permute-start(f32[1,1,136,128]{3,2,1,0:T(8,128)S(1)} %get-tuple-element.56), channel_id=1, source_target_pairs={{0,7},{1,2},{2,1},{3,4},{4,3},{5,6},{6,5},{7,0},{8,15},{9,10},{10,... | collective-permute-start | bytes 208904 | tf_op jit(solution)/shard_map/cond/branch_0_fun/ppermute | solution.py:620
  37.6 0.6 collective-permute-start.8
  38.1 1.6 %branch_0_fun.10 = (f32[1,1,136,128]{3,2,1,0:T(8,128)S(1)}, f32[1,1,136,128]{3,2,1,0:T(8,128)S(1)}, f32[2,128,128]{2,1,0:T(8,128)S(1)}) custom-call(s32[7,3]{1,0:T(8,128)S(1)} %get-tuple-element.40.refs_0_, f32[7,2,128,128]{3,2,1,0:T(8,128)S(1)} %get-tuple-element.58.refs_6_.refs_1_.refs_3_, f32[7,2,128,128]{3,2,1,0:T(8,128)S(1)} %get-tuple-element.49.refs_2_.refs_4_.refs_7_), custom_call_target="tpu_custom_call" | custom-call | flops 2000000000 | bytes 6000000 | tf_op jit(solution)/shard_map/cond/branch_0_fun/pallas_call | solution.py:594
  39.7 1.1 %collective-permute-done.4.refs_2_.refs_13_.refs_15_ = f32[3,1,136,128]{3,2,1,0:T(8,128)S(1)} collective-permute-done((f32[3,1,136,128]{3,2,1,0:T(8,128)S(1)}, f32[3,1,136,128]{3,2,1,0:T(8,128)S(1)}, u32[]{:S(2)}, u32[]{:S(2)}) %collective-permute-start.4) | collective-permute-done | bytes 208928 | tf_op jit(solution)/shard_map/cond/branch_0_fun/ppermute | solution.py:623
  41.7 3.4 %branch_0_fun.11 = (f32[7,2,128,128]{3,2,1,0:T(8,128)S(1)}, f32[2,128,128]{2,1,0:T(8,128)S(1)}, f32[8,128]{1,0:T(8,128)S(1)}, f32[3,1,136,128]{3,2,1,0:T(8,128)S...) custom-call(s32[7,3]{1,0:T(8,128)S(1)} %get-tuple-element.40.refs_0_, ...), custom_call_target="tpu_custom_call" | custom-call | flops 2000000000 | bytes 6000000 | tf_op jit(solution)/shard_map/cond/branch_0_fun/pallas_call | solution.py:594
  45.4 0.5 collective-permute-start.10
  45.9 1.3 %collective-permute-start.14 = (f32[1,1,136,128]{3,2,1,0:T(8,128)S(1)}, f32[1,1,136,128]{3,2,1,0:T(8,128)S(1)}, u32[]{:S(2)}, u32[]{:S(2)}) collective-permute-start(f32[1,1,136,128]{3,2,1,0:T(8,128)S(1)} %get-tuple-element.68), channel_id=1, source_target_pairs={{0,1},{1,0},{2,3},{3,2},{4,5},{5,4},{6,7},{7,6},{8,9},{9,8},{10,11... | collective-permute-start | bytes 208904 | tf_op jit(solution)/shard_map/cond/branch_0_fun/ppermute | solution.py:621
  47.2 3.3 %collective-permute-start.13 = (f32[1,1,136,128]{3,2,1,0:T(8,128)S(1)}, f32[1,1,136,128]{3,2,1,0:T(8,128)S(1)}, u32[]{:S(2)}, u32[]{:S(2)}) collective-permute-start(f32[1,1,136,128]{3,2,1,0:T(8,128)S(1)} %get-tuple-element.68), channel_id=1, source_target_pairs={{0,7},{1,2},{2,1},{3,4},{4,3},{5,6},{6,5},{7,0},{8,15},{9,10},{10,... | collective-permute-start | bytes 208904 | tf_op jit(solution)/shard_map/cond/branch_0_fun/ppermute | solution.py:620
  51.2 2.6 %branch_0_fun.9 = (f32[7,2,128,128]{3,2,1,0:T(8,128)}, f32[8,128]{1,0:T(8,128)S(1)}) custom-call(s32[7,3]{1,0:T(8,128)S(1)} %get-tuple-element.40.refs_0_, s32[3]{0:T(128)S(1)} %get-tuple-element.41.refs_1_, f32[3,1,136,128]{3,2,1,0:T(8,128)S(1)} %collective-permute-done.4.refs_2_.refs_13_.refs_15_, ...), custom_call_target="tpu_custom_call" | custom-call | flops 2000000000 | bytes 6000000 | tf_op jit(solution)/shard_map/cond/branch_0_fun/pallas_call | solution.py:594
  53.8 1.5 %collective-permute-done.11 = f32[8,128]{1,0:T(8,128)S(1)} collective-permute-done((f32[8,128]{1,0:T(8,128)S(1)}, f32[8,128]{1,0:T(8,128)S(1)}, u32[]{:S(2)}, u32[]{:S(2)}) %collective-permute-start.11) | collective-permute-done | bytes 4128 | tf_op jit(solution)/shard_map/cond/branch_0_fun/ppermute | solution.py:644
  55.3 3.7 %branch_0_fun.12 = (f32[7,2,128,128]{3,2,1,0:T(8,128)S(1)}, f32[2,128,128]{2,1,0:T(8,128)S(1)}, f32[8,128]{1,0:T(8,128)S(1)}, f32[2,1,136,128]{3,2,1,0:T(8,128)S...) custom-call(s32[7,3]{1,0:T(8,128)S(1)} %get-tuple-element.40.refs_0_, ...), custom_call_target="tpu_custom_call" | custom-call | flops 2000000000 | bytes 6000000 | tf_op jit(solution)/shard_map/cond/branch_0_fun/pallas_call | solution.py:594
  59.3 3.2 %collective-permute-start.17 = (f32[1,1,136,128]{3,2,1,0:T(8,128)S(1)}, f32[1,1,136,128]{3,2,1,0:T(8,128)S(1)}, u32[]{:S(2)}, u32[]{:S(2)}) collective-permute-start(f32[1,1,136,128]{3,2,1,0:T(8,128)S(1)} %get-tuple-element.76), channel_id=1, source_target_pairs={{0,7},{1,2},{2,1},{3,4},{4,3},{5,6},{6,5},{7,0},{8,15},{9,10},{10,... | collective-permute-start | bytes 208904 | tf_op jit(solution)/shard_map/cond/branch_0_fun/ppermute | solution.py:620
  62.5 1.2 %collective-permute-start.20 = (f32[8,128]{1,0:T(8,128)S(1)}, f32[8,128]{1,0:T(8,128)S(1)}, u32[]{:S(2)}, u32[]{:S(2)}) collective-permute-start(f32[8,128]{1,0:T(8,128)S(1)} %get-tuple-element.78), channel_id=1, source_target_pairs={{0,16},{8,24},{16,0},{24,8},{1,17},{9,25},{17,1},{25,9},{2,18},{10... | collective-permute-start | bytes 12296 | tf_op jit(solution)/shard_map/cond/branch_0_fun/ppermute | solution.py:664
  63.8 0.8 %collective-permute-done.16.refs_6_ = f32[2,1,136,128]{3,2,1,0:T(8,128)S(1)} collective-permute-done((f32[2,1,136,128]{3,2,1,0:T(8,128)S(1)}, f32[2,1,136,128]{3,2,1,0:T(8,128)S(1)}, u32[]{:S(2)}, u32[]{:S(2)}) %collective-permute-start.16) | collective-permute-done | bytes 139296 | tf_op jit(solution)/shard_map/cond/branch_0_fun/ppermute | solution.py:623
  64.6 0.5 collective-permute-done.19.refs_9_
  65.1 1.0 %collective-permute-done.20 = f32[8,128]{1,0:T(8,128)S(1)} collective-permute-done((f32[8,128]{1,0:T(8,128)S(1)}, f32[8,128]{1,0:T(8,128)S(1)}, u32[]{:S(2)}, u32[]{:S(2)}) %collective-permute-start.20) | collective-permute-done | bytes 4128 | tf_op jit(solution)/shard_map/cond/branch_0_fun/ppermute | solution.py:664
  66.1 0.7 collective-permute-done.17.refs_7_
  66.8 3.1 %branch_0_fun.13 = f32[7,2,128,128]{3,2,1,0:T(8,128)} custom-call(s32[7,3]{1,0:T(8,128)S(1)} %get-tuple-element.40.refs_0_, s32[3]{0:T(128)S(1)} %get-tuple-element.41.refs_1_, f32[7,2,128,128]{3,2,1,0:T(8,128)S(1)} %get-tuple-element.73.refs_2_, f32[7,2,128,128]{3,2,1,0:T(8,128)S(1)} %bitcast.62, f32[2,128,128]{2,1,0:T(8,128)S(1)} %get-tuple-element.74.refs_4_, ...), custom_call_target="tpu_custom_call" | custom-call | flops 2000000000 | bytes 6000000 | tf_op jit(solution)/shard_map/cond/branch_0_fun/pallas_call | solution.py:594
  69.9 0.5 fusion.4
  (53 shorter events, 3.3 us)
Async XLA Ops:
  1.4 17.8 %copy-start = (f32[1,1,7,2,128,128]{5,4,3,2,1,0:T(8,128)S(1)}, f32[1,1,7,2,128,128]{5,4,3,2,1,0:T(8,128)}, u32[]{:S(2)}) copy-start(f32[1,1,7,2,128,128]{5,4,3,2,1,0:T(8,128)} %param.7) | copy-start | bytes 2752516
  1.4 17.9 %copy-start.1 = (f32[1,1,7,2,128,128]{5,4,3,2,1,0:T(8,128)S(1)}, f32[1,1,7,2,128,128]{5,4,3,2,1,0:T(8,128)}, u32[]{:S(2)}) copy-start(f32[1,1,7,2,128,128]{5,4,3,2,1,0:T(8,128)} %param.6) | copy-start | bytes 2752516
  4.7 11.6 %collective-permute-start.64 = (f32[3,1,136,128]{3,2,1,0:T(8,128)S(1)}, f32[3,1,136,128]{3,2,1,0:T(8,128)S(1)}, u32[]{:S(2)}, u32[]{:S(2)}) collective-permute-start(f32[3,1,136,128]{3,2,1,0:T(8,128)S(1)} %get-tuple-element.150), channel_id=1, source_target_pairs={{0,24},{8,16},{16,8},{24,0},{1,25},{9,17},{17,9},{25,1},{2,26},{10... | collective-permute-start | bytes 626696 | tf_op jit(solution)/shard_map/ppermute | solution.py:623
  7.2 9.1 %collective-permute-start.65 = (f32[2,1,136,128]{3,2,1,0:T(8,128)S(1)}, f32[2,1,136,128]{3,2,1,0:T(8,128)S(1)}, u32[]{:S(2)}, u32[]{:S(2)}) collective-permute-start(f32[2,1,136,128]{3,2,1,0:T(8,128)S(1)} %get-tuple-element.151), channel_id=1, source_target_pairs={{0,7},{1,2},{2,1},{3,4},{4,3},{5,6},{6,5},{7,0},{8,15},{9,10},{10,... | collective-permute-start | bytes 417800 | tf_op jit(solution)/shard_map/ppermute | solution.py:620
  11.7 7.5 %collective-permute-start.66 = (f32[2,1,136,128]{3,2,1,0:T(8,128)S(1)}, f32[2,1,136,128]{3,2,1,0:T(8,128)S(1)}, u32[]{:S(2)}, u32[]{:S(2)}) collective-permute-start(f32[2,1,136,128]{3,2,1,0:T(8,128)S(1)} %get-tuple-element.151), channel_id=1, source_target_pairs={{0,1},{1,0},{2,3},{3,2},{4,5},{5,4},{6,7},{7,6},{8,9},{9,8},{10,11... | collective-permute-start | bytes 417800 | tf_op jit(solution)/shard_map/ppermute | solution.py:621
  11.7 7.5 %collective-permute-start.67 = (f32[3,1,136,128]{3,2,1,0:T(8,128)S(1)}, f32[3,1,136,128]{3,2,1,0:T(8,128)S(1)}, u32[]{:S(2)}, u32[]{:S(2)}) collective-permute-start(f32[3,1,136,128]{3,2,1,0:T(8,128)S(1)} %get-tuple-element.152), channel_id=1, source_target_pairs={{0,8},{8,0},{16,24},{24,16},{1,9},{9,1},{17,25},{25,17},{2,10},{10... | collective-permute-start | bytes 626696 | tf_op jit(solution)/shard_map/ppermute | solution.py:622
  19.2 0.7 copy-start.2
  22.4 7.6 %collective-permute-start = (f32[2,1,136,128]{3,2,1,0:T(8,128)S(1)}, f32[2,1,136,128]{3,2,1,0:T(8,128)S(1)}, u32[]{:S(2)}, u32[]{:S(2)}) collective-permute-start(f32[2,1,136,128]{3,2,1,0:T(8,128)S(1)} %get-tuple-element.52), channel_id=1, source_target_pairs={{0,24},{8,16},{16,8},{24,0},{1,25},{9,17},{17,9},{25,1},{2,26},{10... | collective-permute-start | bytes 417800 | tf_op jit(solution)/shard_map/cond/branch_0_fun/ppermute | solution.py:623
  22.6 7.4 %collective-permute-start.1 = (f32[1,1,136,128]{3,2,1,0:T(8,128)S(1)}, f32[1,1,136,128]{3,2,1,0:T(8,128)S(1)}, u32[]{:S(2)}, u32[]{:S(2)}) collective-permute-start(f32[1,1,136,128]{3,2,1,0:T(8,128)S(1)} %get-tuple-element.53), channel_id=1, source_target_pairs={{0,7},{1,2},{2,1},{3,4},{4,3},{5,6},{6,5},{7,0},{8,15},{9,10},{10,... | collective-permute-start | bytes 208904 | tf_op jit(solution)/shard_map/cond/branch_0_fun/ppermute | solution.py:620
  24.3 5.8 %collective-permute-start.2 = (f32[1,1,136,128]{3,2,1,0:T(8,128)S(1)}, f32[1,1,136,128]{3,2,1,0:T(8,128)S(1)}, u32[]{:S(2)}, u32[]{:S(2)}) collective-permute-start(f32[1,1,136,128]{3,2,1,0:T(8,128)S(1)} %get-tuple-element.53), channel_id=1, source_target_pairs={{0,1},{1,0},{2,3},{3,2},{4,5},{5,4},{6,7},{7,6},{8,9},{9,8},{10,11... | collective-permute-start | bytes 208904 | tf_op jit(solution)/shard_map/cond/branch_0_fun/ppermute | solution.py:621
  24.3 5.8 %collective-permute-start.3 = (f32[2,1,136,128]{3,2,1,0:T(8,128)S(1)}, f32[2,1,136,128]{3,2,1,0:T(8,128)S(1)}, u32[]{:S(2)}, u32[]{:S(2)}) collective-permute-start(f32[2,1,136,128]{3,2,1,0:T(8,128)S(1)} %get-tuple-element.54), channel_id=1, source_target_pairs={{0,8},{8,0},{16,24},{24,16},{1,9},{9,1},{17,25},{25,17},{2,10},{10... | collective-permute-start | bytes 417800 | tf_op jit(solution)/shard_map/cond/branch_0_fun/ppermute | solution.py:622
  33.4 7.5 %collective-permute-start.4 = (f32[3,1,136,128]{3,2,1,0:T(8,128)S(1)}, f32[3,1,136,128]{3,2,1,0:T(8,128)S(1)}, u32[]{:S(2)}, u32[]{:S(2)}) collective-permute-start(f32[3,1,136,128]{3,2,1,0:T(8,128)S(1)} %get-tuple-element.55), channel_id=1, source_target_pairs={{0,24},{8,16},{16,8},{24,0},{1,25},{9,17},{17,9},{25,1},{2,26},{10... | collective-permute-start | bytes 626696 | tf_op jit(solution)/shard_map/cond/branch_0_fun/ppermute | solution.py:623
  34.0 7.7 %collective-permute-start.6 = (f32[1,1,136,128]{3,2,1,0:T(8,128)S(1)}, f32[1,1,136,128]{3,2,1,0:T(8,128)S(1)}, u32[]{:S(2)}, u32[]{:S(2)}) collective-permute-start(f32[1,1,136,128]{3,2,1,0:T(8,128)S(1)} %get-tuple-element.56), channel_id=1, source_target_pairs={{0,1},{1,0},{2,3},{3,2},{4,5},{5,4},{6,7},{7,6},{8,9},{9,8},{10,11... | collective-permute-start | bytes 208904 | tf_op jit(solution)/shard_map/cond/branch_0_fun/ppermute | solution.py:621
  34.0 7.6 %collective-permute-start.5 = (f32[1,1,136,128]{3,2,1,0:T(8,128)S(1)}, f32[1,1,136,128]{3,2,1,0:T(8,128)S(1)}, u32[]{:S(2)}, u32[]{:S(2)}) collective-permute-start(f32[1,1,136,128]{3,2,1,0:T(8,128)S(1)} %get-tuple-element.56), channel_id=1, source_target_pairs={{0,7},{1,2},{2,1},{3,4},{4,3},{5,6},{6,5},{7,0},{8,15},{9,10},{10,... | collective-permute-start | bytes 208904 | tf_op jit(solution)/shard_map/cond/branch_0_fun/ppermute | solution.py:620
  37.6 3.6 %collective-permute-start.8 = (f32[8,128]{1,0:T(8,128)S(1)}, f32[8,128]{1,0:T(8,128)S(1)}, u32[]{:S(2)}, u32[]{:S(2)}) collective-permute-start(f32[8,128]{1,0:T(8,128)S(1)} %get-tuple-element.61), channel_id=1, source_target_pairs={{0,16},{8,24},{16,0},{24,8},{1,17},{9,25},{17,1},{25,9},{2,18},{10... | collective-permute-start | bytes 12296 | tf_op jit(solution)/shard_map/cond/branch_0_fun/ppermute | solution.py:664
  38.1 2.7 %collective-permute-start.7 = (f32[3,1,136,128]{3,2,1,0:T(8,128)S(1)}, f32[3,1,136,128]{3,2,1,0:T(8,128)S(1)}, u32[]{:S(2)}, u32[]{:S(2)}) collective-permute-start(f32[3,1,136,128]{3,2,1,0:T(8,128)S(1)} %get-tuple-element.57), channel_id=1, source_target_pairs={{0,8},{8,0},{16,24},{24,16},{1,9},{9,1},{17,25},{25,17},{2,10},{10... | collective-permute-start | bytes 626696 | tf_op jit(solution)/shard_map/cond/branch_0_fun/ppermute | solution.py:622
  41.2 4.2 %collective-permute-start.9 = (f32[8,128]{1,0:T(8,128)S(1)}, f32[8,128]{1,0:T(8,128)S(1)}, u32[]{:S(2)}, u32[]{:S(2)}) collective-permute-start(f32[8,128]{1,0:T(8,128)S(1)} %add_add_fusion.1), channel_id=1, source_target_pairs={{0,1},{1,0},{2,3},{3,2},{4,5},{5,4},{6,7},{7,6},{8,9},{9,8},{10,11... | collective-permute-start | bytes 12296 | tf_op jit(solution)/shard_map/cond/branch_0_fun/ppermute | solution.py:644
  45.0 10.2 %collective-permute-start.12 = (f32[3,1,136,128]{3,2,1,0:T(8,128)S(1)}, f32[3,1,136,128]{3,2,1,0:T(8,128)S(1)}, u32[]{:S(2)}, u32[]{:S(2)}) collective-permute-start(f32[3,1,136,128]{3,2,1,0:T(8,128)S(1)} %get-tuple-element.67), channel_id=1, source_target_pairs={{0,24},{8,16},{16,8},{24,0},{1,25},{9,17},{17,9},{25,1},{2,26},{10... | collective-permute-start | bytes 626696 | tf_op jit(solution)/shard_map/cond/branch_0_fun/ppermute | solution.py:623
  45.4 5.3 %collective-permute-start.10 = (f32[8,128]{1,0:T(8,128)S(1)}, f32[8,128]{1,0:T(8,128)S(1)}, u32[]{:S(2)}, u32[]{:S(2)}) collective-permute-start(f32[8,128]{1,0:T(8,128)S(1)} %add_select_fusion), channel_id=1, source_target_pairs={{0,2},{1,3},{2,0},{3,1},{4,6},{5,7},{6,4},{7,5},{8,10},{9,11},{10,... | collective-permute-start | bytes 12296 | tf_op jit(solution)/shard_map/cond/branch_0_fun/ppermute | solution.py:644
  45.9 9.3 %collective-permute-start.14 = (f32[1,1,136,128]{3,2,1,0:T(8,128)S(1)}, f32[1,1,136,128]{3,2,1,0:T(8,128)S(1)}, u32[]{:S(2)}, u32[]{:S(2)}) collective-permute-start(f32[1,1,136,128]{3,2,1,0:T(8,128)S(1)} %get-tuple-element.68), channel_id=1, source_target_pairs={{0,1},{1,0},{2,3},{3,2},{4,5},{5,4},{6,7},{7,6},{8,9},{9,8},{10,11... | collective-permute-start | bytes 208904 | tf_op jit(solution)/shard_map/cond/branch_0_fun/ppermute | solution.py:621
  47.2 8.0 %collective-permute-start.13 = (f32[1,1,136,128]{3,2,1,0:T(8,128)S(1)}, f32[1,1,136,128]{3,2,1,0:T(8,128)S(1)}, u32[]{:S(2)}, u32[]{:S(2)}) collective-permute-start(f32[1,1,136,128]{3,2,1,0:T(8,128)S(1)} %get-tuple-element.68), channel_id=1, source_target_pairs={{0,7},{1,2},{2,1},{3,4},{4,3},{5,6},{6,5},{7,0},{8,15},{9,10},{10,... | collective-permute-start | bytes 208904 | tf_op jit(solution)/shard_map/cond/branch_0_fun/ppermute | solution.py:620
  50.6 4.7 %collective-permute-start.15 = (f32[3,1,136,128]{3,2,1,0:T(8,128)S(1)}, f32[3,1,136,128]{3,2,1,0:T(8,128)S(1)}, u32[]{:S(2)}, u32[]{:S(2)}) collective-permute-start(f32[3,1,136,128]{3,2,1,0:T(8,128)S(1)} %get-tuple-element.72), channel_id=1, source_target_pairs={{0,8},{8,0},{16,24},{24,16},{1,9},{9,1},{17,25},{25,17},{2,10},{10... | collective-permute-start | bytes 626696 | tf_op jit(solution)/shard_map/cond/branch_0_fun/ppermute | solution.py:622
  50.7 4.5 %collective-permute-start.11 = (f32[8,128]{1,0:T(8,128)S(1)}, f32[8,128]{1,0:T(8,128)S(1)}, u32[]{:S(2)}, u32[]{:S(2)}) collective-permute-start(f32[8,128]{1,0:T(8,128)S(1)} %add.120), channel_id=1, source_target_pairs={{0,4},{1,5},{2,6},{3,7},{4,0},{5,1},{6,2},{7,3},{8,12},{9,13},{10,... | collective-permute-start | bytes 12296 | tf_op jit(solution)/shard_map/cond/branch_0_fun/ppermute | solution.py:644
  59.0 5.6 %collective-permute-start.16 = (f32[2,1,136,128]{3,2,1,0:T(8,128)S(1)}, f32[2,1,136,128]{3,2,1,0:T(8,128)S(1)}, u32[]{:S(2)}, u32[]{:S(2)}) collective-permute-start(f32[2,1,136,128]{3,2,1,0:T(8,128)S(1)} %get-tuple-element.75), channel_id=1, source_target_pairs={{0,24},{8,16},{16,8},{24,0},{1,25},{9,17},{17,9},{25,1},{2,26},{10... | collective-permute-start | bytes 417800 | tf_op jit(solution)/shard_map/cond/branch_0_fun/ppermute | solution.py:623
  59.1 7.7 %collective-permute-start.18 = (f32[1,1,136,128]{3,2,1,0:T(8,128)S(1)}, f32[1,1,136,128]{3,2,1,0:T(8,128)S(1)}, u32[]{:S(2)}, u32[]{:S(2)}) collective-permute-start(f32[1,1,136,128]{3,2,1,0:T(8,128)S(1)} %get-tuple-element.76), channel_id=1, source_target_pairs={{0,1},{1,0},{2,3},{3,2},{4,5},{5,4},{6,7},{7,6},{8,9},{9,8},{10,11... | collective-permute-start | bytes 208904 | tf_op jit(solution)/shard_map/cond/branch_0_fun/ppermute | solution.py:621
  59.3 7.5 %collective-permute-start.17 = (f32[1,1,136,128]{3,2,1,0:T(8,128)S(1)}, f32[1,1,136,128]{3,2,1,0:T(8,128)S(1)}, u32[]{:S(2)}, u32[]{:S(2)}) collective-permute-start(f32[1,1,136,128]{3,2,1,0:T(8,128)S(1)} %get-tuple-element.76), channel_id=1, source_target_pairs={{0,7},{1,2},{2,1},{3,4},{4,3},{5,6},{6,5},{7,0},{8,15},{9,10},{10,... | collective-permute-start | bytes 208904 | tf_op jit(solution)/shard_map/cond/branch_0_fun/ppermute | solution.py:620
  62.5 3.6 %collective-permute-start.20 = (f32[8,128]{1,0:T(8,128)S(1)}, f32[8,128]{1,0:T(8,128)S(1)}, u32[]{:S(2)}, u32[]{:S(2)}) collective-permute-start(f32[8,128]{1,0:T(8,128)S(1)} %get-tuple-element.78), channel_id=1, source_target_pairs={{0,16},{8,24},{16,0},{24,8},{1,17},{9,25},{17,1},{25,9},{2,18},{10... | collective-permute-start | bytes 12296 | tf_op jit(solution)/shard_map/cond/branch_0_fun/ppermute | solution.py:664
  63.8 1.4 %collective-permute-start.19 = (f32[2,1,136,128]{3,2,1,0:T(8,128)S(1)}, f32[2,1,136,128]{3,2,1,0:T(8,128)S(1)}, u32[]{:S(2)}, u32[]{:S(2)}) collective-permute-start(f32[2,1,136,128]{3,2,1,0:T(8,128)S(1)} %get-tuple-element.77), channel_id=1, source_target_pairs={{0,8},{8,0},{16,24},{24,16},{1,9},{9,1},{17,25},{25,17},{2,10},{10... | collective-permute-start | bytes 417800 | tf_op jit(solution)/shard_map/cond/branch_0_fun/ppermute | solution.py:622
  66.1 3.8 %collective-permute-start.21 = (f32[8,128]{1,0:T(8,128)S(1)}, f32[8,128]{1,0:T(8,128)S(1)}, u32[]{:S(2)}, u32[]{:S(2)}) collective-permute-start(f32[8,128]{1,0:T(8,128)S(1)} %add_add_fusion), channel_id=1, source_target_pairs={{0,1},{1,0},{2,3},{3,2},{4,5},{5,4},{6,7},{7,6},{8,9},{9,8},{10,11... | collective-permute-start | bytes 12296 | tf_op jit(solution)/shard_map/cond/branch_0_fun/ppermute | solution.py:644
